TPU v7x, 256 devices: a whole 4x4x8 slice. The times are simulated.
256 devices in a mesh: section: 8 (over x, core), dp: 32 (over z, y).
Axes of the slice: x: 4, y: 4, z: 8, core: 2. Of those that a mesh axis runs over, the one named last changes fastest.
Arguments:
- layer_inputs: bfloat16 [8, 5120, 8192], P('section', 'dp'), may hold values from -460 to 460
- queries: bfloat16 [8, 5120, 8192], P('section', 'dp'), may hold values from -9 to 9
- keys: bfloat16 [8, 5120, 512], P('section', 'dp'), may hold values from -4.5 to 4.5
- gains: bfloat16 [8, 8192], P('section'), may hold values from 0.4 to 47
- value_weights: bfloat16 [8, 8192, 512], P('section', 'dp'), may hold values from -0.05634757 to 0.05634757
- out_grad: bfloat16 [5120, 8192], P('dp', 'section'), may hold values from -0.04332382 to 0.04332382
Outputs:
- value_grads: float32 [8, 8192, 512], P('section', 'dp')
All inputs are finite; a program needn't handle non-finite values.
Results may differ from a plain program's by a relative error of at most 0.03.
Values may be sent and summed in bfloat16 or wider, within the bound.
A program may use at most 192 MiB of HBM per device.

v0:
```python
import jax
import jax.numpy as jnp
from jax import lax
from jax.sharding import PartitionSpec as P

QH = 64
KVH = 4
HD = 128
MB_TOK = 80


EPSILON = 1e-05


def passed_along(block, axis, distance):
    devices = range(lax.axis_size(axis))
    route = [(i - distance, i) for i in devices if i - distance in devices]
    return lax.ppermute(block, axis, route)


def recompute(rows_in, rows_query, rows_key, gain_rows, weights, upstream):
    row_count = rows_in.shape[0]
    sequences = row_count // MB_TOK
    per_group = QH // KVH
    floats = rows_in.astype(jnp.float32)
    inverse = lax.rsqrt(jnp.mean(floats * floats, axis=-1, keepdims=True) + EPSILON)
    normed = floats * inverse
    hidden = (normed * gain_rows).astype(jnp.bfloat16)
    query_rows = rows_query.reshape(sequences, MB_TOK, KVH, per_group, HD)
    key_rows = rows_key.reshape(sequences, MB_TOK, KVH, HD)
    scores = jnp.einsum(
        "btgqd,bsgd->bgqts", query_rows, key_rows, preferred_element_type=jnp.float32
    ) * HD ** (-0.5)
    causal = jnp.arange(MB_TOK)[:, None] >= jnp.arange(MB_TOK)[None, :]
    scores = jnp.where(causal, scores, -jnp.inf)
    row_max = jnp.max(scores, axis=-1, keepdims=True)
    exponent = jnp.exp(scores - row_max)
    probabilities = (exponent / jnp.sum(exponent, axis=-1, keepdims=True)).astype(jnp.bfloat16)
    upstream_heads = upstream.reshape(sequences, MB_TOK, KVH, per_group, HD)
    value_grad = jnp.einsum(
        "bgqts,btgqd->bsgd", probabilities, upstream_heads, preferred_element_type=jnp.float32
    )
    value_grad = value_grad.reshape(row_count, KVH * HD).astype(jnp.bfloat16)
    hidden_grad = lax.dot_general(
        value_grad, weights, (((1,), (1,)), ((), ())), preferred_element_type=jnp.float32
    )
    scaled = hidden_grad * gain_rows
    inner_mean = jnp.mean(scaled * normed, axis=-1, keepdims=True)
    outgoing = (upstream.astype(jnp.float32) + inverse * (scaled - normed * inner_mean)).astype(
        jnp.bfloat16
    )
    return (outgoing, value_grad, hidden)


def shards(layer_inputs, queries, keys, gains, value_weights, out_grad):
    sections = lax.axis_size("section")
    my_section = lax.axis_index("section")
    final_section = sections - 1
    top_grad = lax.all_gather(out_grad, "section", axis=1, tiled=True)
    weights = lax.all_gather(value_weights[0], "dp", axis=0, tiled=True)
    rows_in = layer_inputs[0]
    rows_query = queries[0]
    rows_key = keys[0]
    gain_rows = gains[0].astype(jnp.float32)
    token_count = rows_in.shape[0]
    width = rows_in.shape[1]
    kv_width = rows_key.shape[1]
    blocks_held = token_count // MB_TOK
    turns = final_section + blocks_held
    partial_shape = (width, kv_width)

    def spare_block(upstream):
        return (
            jnp.zeros((MB_TOK, width), jnp.bfloat16),
            jnp.zeros((MB_TOK, kv_width), jnp.bfloat16),
            jnp.zeros((MB_TOK, width), jnp.bfloat16),
            jnp.zeros(partial_shape, jnp.float32),
        )

    def turn(turn_index, carry):
        incoming, grad_rows, hidden_rows, running = carry
        block_index = turn_index - (final_section - my_section)
        active = jnp.logical_and(block_index >= 0, block_index < blocks_held)
        row_start = jnp.clip(block_index, 0, blocks_held - 1) * MB_TOK
        upstream = jnp.where(
            my_section == final_section,
            lax.dynamic_slice_in_dim(top_grad, row_start, MB_TOK, 0),
            incoming,
        )

        def run_block(rows):
            outgoing, value_grad, hidden = recompute(
                lax.dynamic_slice_in_dim(rows_in, row_start, MB_TOK, 0),
                lax.dynamic_slice_in_dim(rows_query, row_start, MB_TOK, 0),
                lax.dynamic_slice_in_dim(rows_key, row_start, MB_TOK, 0),
                gain_rows,
                weights,
                rows,
            )
            partial_value = jnp.einsum(
                "td,tk->dk", hidden, value_grad, preferred_element_type=jnp.float32
            )
            return (outgoing, value_grad, hidden, partial_value)

        outgoing, value_grad, hidden, partial_value = lax.cond(
            active, run_block, spare_block, upstream
        )
        kept_grad = lax.dynamic_slice_in_dim(grad_rows, row_start, MB_TOK, 0)
        grad_rows = lax.dynamic_update_slice_in_dim(
            grad_rows, jnp.where(active, value_grad, kept_grad), row_start, 0
        )
        kept_hidden = lax.dynamic_slice_in_dim(hidden_rows, row_start, MB_TOK, 0)
        hidden_rows = lax.dynamic_update_slice_in_dim(
            hidden_rows, jnp.where(active, hidden, kept_hidden), row_start, 0
        )
        incoming = passed_along(outgoing, "section", -1)
        return (incoming, grad_rows, hidden_rows, running + partial_value)

    initial = (
        jnp.zeros((MB_TOK, width), jnp.bfloat16),
        jnp.zeros((token_count, kv_width), jnp.bfloat16),
        jnp.zeros((token_count, width), jnp.bfloat16),
        jnp.zeros(partial_shape, jnp.float32),
    )
    final_carry = lax.fori_loop(0, turns, turn, initial)
    grad_rows = final_carry[1]
    hidden_rows = final_carry[2]
    running = final_carry[3]
    owned_rows = lax.psum_scatter(
        running.astype(jnp.bfloat16), "dp", scatter_dimension=0, tiled=True
    ).astype(jnp.float32)
    square_sum = lax.psum(jnp.sum(owned_rows * owned_rows), ("section", "dp"))
    ceiling = jnp.sqrt(jnp.float32(sections * width * kv_width))
    factor = jnp.minimum(1.0, ceiling / jnp.sqrt(square_sum))
    return (owned_rows * factor)[None]


def solution(mesh):
    return jax.shard_map(
        shards,
        mesh=mesh,
        in_specs=(
            P("section", "dp", None),
            P("section", "dp", None),
            P("section", "dp", None),
            P("section", None),
            P("section", "dp", None),
            P("dp", "section"),
        ),
        out_specs=P("section", "dp", None),
        check_vma=False,
    )
```

profile of v0, /device:TPU:1, one launch (start us, length us, event | category | flops | bytes accessed | tf_op | source)
XLA Modules:
  0.0 810.6 jit_solution(11578485062493066715)
XLA Ops:
  8.9 33.2 %all-gather.4.cloned.1.call-done = bf16[160,8192]{1,0:T(8,128)(2,1)} async-done(((bf16[160,1024]{1,0:T(8,128)(2,1)}), bf16[160,8192]{1,0:T(8,128)(2,1)}) %all-gather.4.cloned.1.call-update) | async-done | bytes 2621456 | tf_op jit(solution)/shard_map/all_gather | solution.py:59
  42.1 100.9 %all-gather.6.cloned.1.call-done = bf16[1,8192,512]{2,1,0:T(8,128)(2,1)} async-done(((bf16[1,256,512]{2,1,0:T(8,128)(2,1)}), bf16[1,8192,512]{2,1,0:T(8,128)(2,1)}) %all-gather.6.cloned.1.call-update) | async-done | bytes 8388624 | tf_op jit(solution)/shard_map/all_gather | solution.py:60
  143.1 349.7 %while.18 = (s32[]{:T(128)}, bf16[80,8192]{1,0:T(8,128)(2,1)S(1)}, f32[8192,512]{1,0:T(8,128)}, s32[]{:T(128)}, pred[]{:T(512)}, /*index=5*/bf16[160,8192]{1,0:T...) while((s32[]{:T(128)}, bf16[80,8192]{1,0:T(8,128)(2,1)S(1)}, ...), condition=%wide.region_7.8_spmd.clone, body=%wide.region_0.7_spmd.clone.sunk | while | flops 1579651328 | bytes 168854400 | solution.py:125
  143.1 9.1 %conditional.3 = (bf16[80,8192]{1,0:T(8,128)(2,1)}, f32[8192,512]{1,0:T(8,128)}) conditional(s32[]{:T(128)} %convert_element_type.106, () %tuple.63, (pred[]{:T(512)}, s32[]{:T(128)}, bf16[160,8192]{1,0:T(8,128)(2,1)}, bf16[80,8192]{1,0:T(8,128)(2,1)S(1)}, bf16[160,8192]{1,0:T(8,128)(2,1)}, /*index=5*/bf16[160,512]{1,0:T(8,128)(2,1)}, ...), branch_computations={%region_1.1_spmd, %region_2.6_spmd} | conditional | flops 1571262720 | bytes 113279568 | solution.py:105
  143.2 7.9 broadcast.47
  151.0 1.2 broadcast.46
  152.2 3.0 collective-permute-start
  155.2 12.6 %select_add_fusion.2 = f32[8192,512]{1,0:T(8,128)} fusion(f32[8192,512]{1,0:T(8,128)} %get-tuple-element.477, f32[8192,512]{1,0:T(8,128)} %get-tuple-element.498, pred[]{:T(512)S(6)} %compare.3), kind=kLoop, calls=%fused_computation.41.clone.1 | loop fusion | flops 8388608 | bytes 50331648 | tf_op jit(solution)/shard_map/while/body/eval_jaxpr/add | solution.py:117
  167.8 3.9 collective-permute-done
  171.8 9.1 %conditional.3 = (bf16[80,8192]{1,0:T(8,128)(2,1)}, f32[8192,512]{1,0:T(8,128)}) conditional(s32[]{:T(128)} %convert_element_type.106, () %tuple.63, (pred[]{:T(512)}, s32[]{:T(128)}, bf16[160,8192]{1,0:T(8,128)(2,1)}, bf16[80,8192]{1,0:T(8,128)(2,1)S(1)}, bf16[160,8192]{1,0:T(8,128)(2,1)}, /*index=5*/bf16[160,512]{1,0:T(8,128)(2,1)}, ...), branch_computations={%region_1.1_spmd, %region_2.6_spmd} | conditional | flops 1571262720 | bytes 113279568 | solution.py:105
  171.8 7.9 broadcast.47
  179.6 1.2 broadcast.46
  180.8 1.9 collective-permute-start
  182.7 17.5 %select_add_fusion.2 = f32[8192,512]{1,0:T(8,128)} fusion(f32[8192,512]{1,0:T(8,128)} %get-tuple-element.477, f32[8192,512]{1,0:T(8,128)} %get-tuple-element.498, pred[]{:T(512)S(6)} %compare.3), kind=kLoop, calls=%fused_computation.41.clone.1 | loop fusion | flops 8388608 | bytes 50331648 | tf_op jit(solution)/shard_map/while/body/eval_jaxpr/add | solution.py:117
  200.3 9.1 %conditional.3 = (bf16[80,8192]{1,0:T(8,128)(2,1)}, f32[8192,512]{1,0:T(8,128)}) conditional(s32[]{:T(128)} %convert_element_type.106, () %tuple.63, (pred[]{:T(512)}, s32[]{:T(128)}, bf16[160,8192]{1,0:T(8,128)(2,1)}, bf16[80,8192]{1,0:T(8,128)(2,1)S(1)}, bf16[160,8192]{1,0:T(8,128)(2,1)}, /*index=5*/bf16[160,512]{1,0:T(8,128)(2,1)}, ...), branch_computations={%region_1.1_spmd, %region_2.6_spmd} | conditional | flops 1571262720 | bytes 113279568 | solution.py:105
  200.3 7.9 broadcast.47
  208.2 1.2 broadcast.46
  209.3 1.9 collective-permute-start
  211.3 17.5 %select_add_fusion.2 = f32[8192,512]{1,0:T(8,128)} fusion(f32[8192,512]{1,0:T(8,128)} %get-tuple-element.477, f32[8192,512]{1,0:T(8,128)} %get-tuple-element.498, pred[]{:T(512)S(6)} %compare.3), kind=kLoop, calls=%fused_computation.41.clone.1 | loop fusion | flops 8388608 | bytes 50331648 | tf_op jit(solution)/shard_map/while/body/eval_jaxpr/add | solution.py:117
  228.8 9.1 %conditional.3 = (bf16[80,8192]{1,0:T(8,128)(2,1)}, f32[8192,512]{1,0:T(8,128)}) conditional(s32[]{:T(128)} %convert_element_type.106, () %tuple.63, (pred[]{:T(512)}, s32[]{:T(128)}, bf16[160,8192]{1,0:T(8,128)(2,1)}, bf16[80,8192]{1,0:T(8,128)(2,1)S(1)}, bf16[160,8192]{1,0:T(8,128)(2,1)}, /*index=5*/bf16[160,512]{1,0:T(8,128)(2,1)}, ...), branch_computations={%region_1.1_spmd, %region_2.6_spmd} | conditional | flops 1571262720 | bytes 113279568 | solution.py:105
  228.8 7.9 broadcast.47
  236.7 1.2 broadcast.46
  237.8 1.9 collective-permute-start
  239.8 17.5 %select_add_fusion.2 = f32[8192,512]{1,0:T(8,128)} fusion(f32[8192,512]{1,0:T(8,128)} %get-tuple-element.477, f32[8192,512]{1,0:T(8,128)} %get-tuple-element.498, pred[]{:T(512)S(6)} %compare.3), kind=kLoop, calls=%fused_computation.41.clone.1 | loop fusion | flops 8388608 | bytes 50331648 | tf_op jit(solution)/shard_map/while/body/eval_jaxpr/add | solution.py:117
  257.3 9.1 %conditional.3 = (bf16[80,8192]{1,0:T(8,128)(2,1)}, f32[8192,512]{1,0:T(8,128)}) conditional(s32[]{:T(128)} %convert_element_type.106, () %tuple.63, (pred[]{:T(512)}, s32[]{:T(128)}, bf16[160,8192]{1,0:T(8,128)(2,1)}, bf16[80,8192]{1,0:T(8,128)(2,1)S(1)}, bf16[160,8192]{1,0:T(8,128)(2,1)}, /*index=5*/bf16[160,512]{1,0:T(8,128)(2,1)}, ...), branch_computations={%region_1.1_spmd, %region_2.6_spmd} | conditional | flops 1571262720 | bytes 113279568 | solution.py:105
  257.3 7.9 broadcast.47
  265.2 1.2 broadcast.46
  266.4 1.9 collective-permute-start
  268.3 17.5 %select_add_fusion.2 = f32[8192,512]{1,0:T(8,128)} fusion(f32[8192,512]{1,0:T(8,128)} %get-tuple-element.477, f32[8192,512]{1,0:T(8,128)} %get-tuple-element.498, pred[]{:T(512)S(6)} %compare.3), kind=kLoop, calls=%fused_computation.41.clone.1 | loop fusion | flops 8388608 | bytes 50331648 | tf_op jit(solution)/shard_map/while/body/eval_jaxpr/add | solution.py:117
  285.8 9.1 %conditional.3 = (bf16[80,8192]{1,0:T(8,128)(2,1)}, f32[8192,512]{1,0:T(8,128)}) conditional(s32[]{:T(128)} %convert_element_type.106, () %tuple.63, (pred[]{:T(512)}, s32[]{:T(128)}, bf16[160,8192]{1,0:T(8,128)(2,1)}, bf16[80,8192]{1,0:T(8,128)(2,1)S(1)}, bf16[160,8192]{1,0:T(8,128)(2,1)}, /*index=5*/bf16[160,512]{1,0:T(8,128)(2,1)}, ...), branch_computations={%region_1.1_spmd, %region_2.6_spmd} | conditional | flops 1571262720 | bytes 113279568 | solution.py:105
  285.8 7.9 broadcast.47
  293.7 1.2 broadcast.46
  294.9 1.9 collective-permute-start
  296.8 17.5 %select_add_fusion.2 = f32[8192,512]{1,0:T(8,128)} fusion(f32[8192,512]{1,0:T(8,128)} %get-tuple-element.477, f32[8192,512]{1,0:T(8,128)} %get-tuple-element.498, pred[]{:T(512)S(6)} %compare.3), kind=kLoop, calls=%fused_computation.41.clone.1 | loop fusion | flops 8388608 | bytes 50331648 | tf_op jit(solution)/shard_map/while/body/eval_jaxpr/add | solution.py:117
  314.3 55.9 %collective-permute-done = bf16[80,8192]{1,0:T(8,128)(2,1)S(1)} collective-permute-done((bf16[80,8192]{1,0:T(8,128)(2,1)}, bf16[80,8192]{1,0:T(8,128)(2,1)S(1)}, u32[]{:S(2)}, u32[]{:S(2)}) %collective-permute-start) | collective-permute-done | bytes 1310752 | tf_op jit(solution)/shard_map/while/body/eval_jaxpr/ppermute | solution.py:18
  370.2 26.2 %conditional.3 = (bf16[80,8192]{1,0:T(8,128)(2,1)}, f32[8192,512]{1,0:T(8,128)}) conditional(s32[]{:T(128)} %convert_element_type.106, () %tuple.63, (pred[]{:T(512)}, s32[]{:T(128)}, bf16[160,8192]{1,0:T(8,128)(2,1)}, bf16[80,8192]{1,0:T(8,128)(2,1)S(1)}, bf16[160,8192]{1,0:T(8,128)(2,1)}, /*index=5*/bf16[160,512]{1,0:T(8,128)(2,1)}, ...), branch_computations={%region_1.1_spmd, %region_2.6_spmd} | conditional | flops 1571262720 | bytes 113279568 | solution.py:105
  370.2 3.2 dynamic-slice_bitcast_fusion
  374.4 1.8 fusion.11
  377.8 2.8 copy.14
  380.6 1.8 copy.17
  383.5 8.2 %fusion.12 = f32[8192,512]{1,0:T(8,128)} fusion(f32[8192]{0:T(1024)S(1)} %get-tuple-element.324, f32[80]{0:T(128)S(1)} %add_rsqrt_fusion, bf16[160,8192]{1,0:T(8,128)(2,1)S(1)} %copy-done, s32[]{:T(128)S(6)} %select_n.44, bf16[10,8,4,128]{3,2,1,0:T(4,128)(2,1)S(1)} %bitcast.58), kind=kOutput, calls=%fused_computation.18 | convolution fusion | flops 673710080 | bytes 18203140 | tf_op jit(solution)/shard_map/while/body/eval_jaxpr/cond/branch_1_fun/td,tk->dk/dot_general | solution.py:100
  391.7 2.7 fusion.3
  394.5 1.9 fusion.7
  396.4 1.9 collective-permute-start
  398.3 17.5 %select_add_fusion.2 = f32[8192,512]{1,0:T(8,128)} fusion(f32[8192,512]{1,0:T(8,128)} %get-tuple-element.477, f32[8192,512]{1,0:T(8,128)} %get-tuple-element.498, pred[]{:T(512)S(6)} %compare.3), kind=kLoop, calls=%fused_computation.41.clone.1 | loop fusion | flops 8388608 | bytes 50331648 | tf_op jit(solution)/shard_map/while/body/eval_jaxpr/add | solution.py:117
  415.9 26.2 %conditional.3 = (bf16[80,8192]{1,0:T(8,128)(2,1)}, f32[8192,512]{1,0:T(8,128)}) conditional(s32[]{:T(128)} %convert_element_type.106, () %tuple.63, (pred[]{:T(512)}, s32[]{:T(128)}, bf16[160,8192]{1,0:T(8,128)(2,1)}, bf16[80,8192]{1,0:T(8,128)(2,1)S(1)}, bf16[160,8192]{1,0:T(8,128)(2,1)}, /*index=5*/bf16[160,512]{1,0:T(8,128)(2,1)}, ...), branch_computations={%region_1.1_spmd, %region_2.6_spmd} | conditional | flops 1571262720 | bytes 113279568 | solution.py:105
  415.9 3.2 dynamic-slice_bitcast_fusion
  420.1 1.8 fusion.11
  423.4 2.8 copy.14
  426.2 1.8 copy.17
  429.1 8.2 %fusion.12 = f32[8192,512]{1,0:T(8,128)} fusion(f32[8192]{0:T(1024)S(1)} %get-tuple-element.324, f32[80]{0:T(128)S(1)} %add_rsqrt_fusion, bf16[160,8192]{1,0:T(8,128)(2,1)S(1)} %copy-done, s32[]{:T(128)S(6)} %select_n.44, bf16[10,8,4,128]{3,2,1,0:T(4,128)(2,1)S(1)} %bitcast.58), kind=kOutput, calls=%fused_computation.18 | convolution fusion | flops 673710080 | bytes 18203140 | tf_op jit(solution)/shard_map/while/body/eval_jaxpr/cond/branch_1_fun/td,tk->dk/dot_general | solution.py:100
  437.4 2.7 fusion.3
  440.1 1.9 fusion.7
  442.0 1.9 collective-permute-start
  444.0 17.5 %select_add_fusion.2 = f32[8192,512]{1,0:T(8,128)} fusion(f32[8192,512]{1,0:T(8,128)} %get-tuple-element.477, f32[8192,512]{1,0:T(8,128)} %get-tuple-element.498, pred[]{:T(512)S(6)} %compare.3), kind=kLoop, calls=%fused_computation.41.clone.1 | loop fusion | flops 8388608 | bytes 50331648 | tf_op jit(solution)/shard_map/while/body/eval_jaxpr/add | solution.py:117
  461.5 9.1 %conditional.3 = (bf16[80,8192]{1,0:T(8,128)(2,1)}, f32[8192,512]{1,0:T(8,128)}) conditional(s32[]{:T(128)} %convert_element_type.106, () %tuple.63, (pred[]{:T(512)}, s32[]{:T(128)}, bf16[160,8192]{1,0:T(8,128)(2,1)}, bf16[80,8192]{1,0:T(8,128)(2,1)S(1)}, bf16[160,8192]{1,0:T(8,128)(2,1)}, /*index=5*/bf16[160,512]{1,0:T(8,128)(2,1)}, ...), branch_computations={%region_1.1_spmd, %region_2.6_spmd} | conditional | flops 1571262720 | bytes 113279568 | solution.py:105
  461.5 7.9 broadcast.47
  470.6 4.7 collective-permute-start
  475.3 17.5 %select_add_fusion.2 = f32[8192,512]{1,0:T(8,128)} fusion(f32[8192,512]{1,0:T(8,128)} %get-tuple-element.477, f32[8192,512]{1,0:T(8,128)} %get-tuple-element.498, pred[]{:T(512)S(6)} %compare.3), kind=kLoop, calls=%fused_computation.41.clone.1 | loop fusion | flops 8388608 | bytes 50331648 | tf_op jit(solution)/shard_map/while/body/eval_jaxpr/add | solution.py:117
  492.8 9.0 %convert_element_type.62 = bf16[8192,512]{1,0:T(8,128)(2,1)} convert(f32[8192,512]{1,0:T(8,128)} %get-tuple-element.340) | non-fusion elementwise | flops 4194304 | bytes 25165824 | tf_op jit(solution)/shard_map/convert_element_type | solution.py:130
  501.8 219.6 %reduce-scatter.2.cloned.1.call-done = bf16[256,512]{1,0:T(8,128)(2,1)} async-done(((bf16[8192,512]{1,0:T(8,128)(2,1)}), bf16[256,512]{1,0:T(8,128)(2,1)}) %reduce-scatter.2.cloned.1.call-update) | async-done | bytes 262160 | tf_op jit(solution)/shard_map/reduce_scatter | solution.py:129
  721.5 1.7 fusion.29
  723.1 78.4 %psum.7 = f32[]{:T(128)} all-reduce(f32[]{:T(128)} %fusion.29), channel_id=1, replica_groups=mesh['section'=8,'dp'=32] {'section','dp'}, use_global_device_ids=true, to_apply=%region_10.11 | all-reduce | flops 1 | bytes 8 | tf_op jit(solution)/shard_map/psum | solution.py:132
  802.2 1.8 fusion.30
  (65 shorter events, 10.9 us)
Async XLA Ops:
  6.5 35.6 %all-gather.4.cloned.1.call-start = ((), (), s32[]{:S(2)}) async-start(), calls=%async_computation.1 | async-start | bytes 2949120 | tf_op jit(solution)/shard_map/all_gather | solution.py:59
  7.3 135.8 %all-gather.6.cloned.1.call-start = ((), (), s32[]{:S(2)}) async-start(), calls=%async_computation.3 | async-start | bytes 8650752 | tf_op jit(solution)/shard_map/all_gather | solution.py:60
  8.0 713.4 %reduce-scatter.2.cloned.1.call-start = ((), (), s32[]{:S(2)}) async-start(), calls=%async_computation.2 | async-start | bytes 8650752 | tf_op jit(solution)/shard_map/reduce_scatter | solution.py:129
  152.2 19.6 %collective-permute-start = (bf16[80,8192]{1,0:T(8,128)(2,1)}, bf16[80,8192]{1,0:T(8,128)(2,1)S(1)}, u32[]{:S(2)}, u32[]{:S(2)}) collective-permute-start(bf16[80,8192]{1,0:T(8,128)(2,1)} %get-tuple-element.476), channel_id=1, source_target_pairs={{32,0},{64,32},{96,64},{128,96},{160,128},{192,160},{224,192},{33,... | collective-permute-start | bytes 3932168 | tf_op jit(solution)/shard_map/while/body/eval_jaxpr/ppermute | solution.py:18
  180.8 19.5 %collective-permute-start = (bf16[80,8192]{1,0:T(8,128)(2,1)}, bf16[80,8192]{1,0:T(8,128)(2,1)S(1)}, u32[]{:S(2)}, u32[]{:S(2)}) collective-permute-start(bf16[80,8192]{1,0:T(8,128)(2,1)} %get-tuple-element.476), channel_id=1, source_target_pairs={{32,0},{64,32},{96,64},{128,96},{160,128},{192,160},{224,192},{33,... | collective-permute-start | bytes 3932168 | tf_op jit(solution)/shard_map/while/body/eval_jaxpr/ppermute | solution.py:18
  209.3 19.5 %collective-permute-start = (bf16[80,8192]{1,0:T(8,128)(2,1)}, bf16[80,8192]{1,0:T(8,128)(2,1)S(1)}, u32[]{:S(2)}, u32[]{:S(2)}) collective-permute-start(bf16[80,8192]{1,0:T(8,128)(2,1)} %get-tuple-element.476), channel_id=1, source_target_pairs={{32,0},{64,32},{96,64},{128,96},{160,128},{192,160},{224,192},{33,... | collective-permute-start | bytes 3932168 | tf_op jit(solution)/shard_map/while/body/eval_jaxpr/ppermute | solution.py:18
  237.8 19.5 %collective-permute-start = (bf16[80,8192]{1,0:T(8,128)(2,1)}, bf16[80,8192]{1,0:T(8,128)(2,1)S(1)}, u32[]{:S(2)}, u32[]{:S(2)}) collective-permute-start(bf16[80,8192]{1,0:T(8,128)(2,1)} %get-tuple-element.476), channel_id=1, source_target_pairs={{32,0},{64,32},{96,64},{128,96},{160,128},{192,160},{224,192},{33,... | collective-permute-start | bytes 3932168 | tf_op jit(solution)/shard_map/while/body/eval_jaxpr/ppermute | solution.py:18
  266.4 19.5 %collective-permute-start = (bf16[80,8192]{1,0:T(8,128)(2,1)}, bf16[80,8192]{1,0:T(8,128)(2,1)S(1)}, u32[]{:S(2)}, u32[]{:S(2)}) collective-permute-start(bf16[80,8192]{1,0:T(8,128)(2,1)} %get-tuple-element.476), channel_id=1, source_target_pairs={{32,0},{64,32},{96,64},{128,96},{160,128},{192,160},{224,192},{33,... | collective-permute-start | bytes 3932168 | tf_op jit(solution)/shard_map/while/body/eval_jaxpr/ppermute | solution.py:18
  294.9 75.3 %collective-permute-start = (bf16[80,8192]{1,0:T(8,128)(2,1)}, bf16[80,8192]{1,0:T(8,128)(2,1)S(1)}, u32[]{:S(2)}, u32[]{:S(2)}) collective-permute-start(bf16[80,8192]{1,0:T(8,128)(2,1)} %get-tuple-element.476), channel_id=1, source_target_pairs={{32,0},{64,32},{96,64},{128,96},{160,128},{192,160},{224,192},{33,... | collective-permute-start | bytes 3932168 | tf_op jit(solution)/shard_map/while/body/eval_jaxpr/ppermute | solution.py:18
  373.4 0.9 copy-start.3
  380.6 1.8 copy-start.1
  380.6 2.5 copy-start
  383.1 8.6 %slice-start = ((s8[8388608]{0:T(1024)(128)(4,1)}), s8[4194304]{0:T(1024)(128)(4,1)S(1)}, s32[]{:S(2)}) async-start(s8[8388608]{0:T(1024)(128)(4,1)} %bitcast.54), calls=%async_computation.4 | async-start | bytes 8388608 | tf_op jit(solution)/shard_map/while/body/eval_jaxpr/cond
  383.5 8.2 %slice-start.1 = ((s8[8388608]{0:T(1024)(128)(4,1)}), s8[4194304]{0:T(1024)(128)(4,1)S(1)}, s32[]{:S(2)}) async-start(s8[8388608]{0:T(1024)(128)(4,1)} %bitcast.54), calls=%async_computation.5 | async-start | bytes 8388608 | tf_op jit(solution)/shard_map/while/body/eval_jaxpr/cond
  391.7 2.8 copy-start.2
  396.4 19.5 %collective-permute-start = (bf16[80,8192]{1,0:T(8,128)(2,1)}, bf16[80,8192]{1,0:T(8,128)(2,1)S(1)}, u32[]{:S(2)}, u32[]{:S(2)}) collective-permute-start(bf16[80,8192]{1,0:T(8,128)(2,1)} %get-tuple-element.476), channel_id=1, source_target_pairs={{32,0},{64,32},{96,64},{128,96},{160,128},{192,160},{224,192},{33,... | collective-permute-start | bytes 3932168 | tf_op jit(solution)/shard_map/while/body/eval_jaxpr/ppermute | solution.py:18
  419.1 0.9 copy-start.3
  426.2 1.8 copy-start.1
  426.2 2.5 copy-start
  428.8 8.6 %slice-start = ((s8[8388608]{0:T(1024)(128)(4,1)}), s8[4194304]{0:T(1024)(128)(4,1)S(1)}, s32[]{:S(2)}) async-start(s8[8388608]{0:T(1024)(128)(4,1)} %bitcast.54), calls=%async_computation.4 | async-start | bytes 8388608 | tf_op jit(solution)/shard_map/while/body/eval_jaxpr/cond
  429.1 8.2 %slice-start.1 = ((s8[8388608]{0:T(1024)(128)(4,1)}), s8[4194304]{0:T(1024)(128)(4,1)S(1)}, s32[]{:S(2)}) async-start(s8[8388608]{0:T(1024)(128)(4,1)} %bitcast.54), calls=%async_computation.5 | async-start | bytes 8388608 | tf_op jit(solution)/shard_map/while/body/eval_jaxpr/cond
  437.3 2.8 copy-start.2
  442.0 19.5 %collective-permute-start = (bf16[80,8192]{1,0:T(8,128)(2,1)}, bf16[80,8192]{1,0:T(8,128)(2,1)S(1)}, u32[]{:S(2)}, u32[]{:S(2)}) collective-permute-start(bf16[80,8192]{1,0:T(8,128)(2,1)} %get-tuple-element.476), channel_id=1, source_target_pairs={{32,0},{64,32},{96,64},{128,96},{160,128},{192,160},{224,192},{33,... | collective-permute-start | bytes 3932168 | tf_op jit(solution)/shard_map/while/body/eval_jaxpr/ppermute | solution.py:18
  470.6 22.3 %collective-permute-start = (bf16[80,8192]{1,0:T(8,128)(2,1)}, bf16[80,8192]{1,0:T(8,128)(2,1)S(1)}, u32[]{:S(2)}, u32[]{:S(2)}) collective-permute-start(bf16[80,8192]{1,0:T(8,128)(2,1)} %get-tuple-element.476), channel_id=1, source_target_pairs={{32,0},{64,32},{96,64},{128,96},{160,128},{192,160},{224,192},{33,... | collective-permute-start | bytes 3932168 | tf_op jit(solution)/shard_map/while/body/eval_jaxpr/ppermute | solution.py:18
Sparse Core Ops, SparseCore 0:
  9.2 32.8 all-gather.3
  44.7 98.2 all-gather.5
  502.0 219.4 reduce-scatter.1
where the time goes:
time: 811 us
  waiting for transfers between devices  415 us (51%)
  other arithmetic  180 us (22%)
  blocking collectives  78.4 us (10%)
  local copies, waits for them, and re-layouts  74.8 us (9%)
  matrix products  26.6 us (3%)
  starting transfers between devices  21.1 us (3%)
  between operations  13.8 us (2%)
    reduce_scatter x1, waiting for transfers between devices, shards(): lax.psum_scatter(running.astype(jnp.bfloat16), 'dp', scatter_dimension=0,...  220 us
    add x9, other arithmetic, turn(): return (incoming, grad_rows, hidden_rows, running + partial_value)  153 us
    all_gather x1, waiting for transfers between devices, shards(): weights = lax.all_gather(value_weights[0], 'dp', axis=0, tiled=True)  101 us
    psum x1, blocking collectives, shards(): square_sum = lax.psum(jnp.sum(owned_rows * owned_rows), ('section', 'dp'))  78.4 us
    another operation x19, local copies, waits for them, and re-layouts  69.1 us
    ppermute x9, waiting for transfers between devices, passed_along(): return lax.ppermute(block, axis, route)  59.8 us
    all_gather x1, waiting for transfers between devices, shards(): top_grad = lax.all_gather(out_grad, 'section', axis=1, tiled=True)  33.2 us
    ppermute x9, starting transfers between devices, passed_along(): return lax.ppermute(block, axis, route)  21 us
  transfers between devices with their start and end apart: 12, of which 5 were waited for; matrix products, arithmetic and copies ran while one was open for 19% of the time, Pallas kernels for 0%

commit v1 on v0

v1 whole, which is shorter than its diff:
```python
import jax
import jax.numpy as jnp
from jax import lax
from jax.experimental import pallas as pl
from jax.experimental.pallas import tpu as pltpu
from jax.sharding import PartitionSpec as P

MESH = pl.DeviceIdType.MESH
F32, BF16 = jnp.float32, jnp.bfloat16
QH, KVH, HD, SEQ, D = 64, 4, 128, 80, 8192
PER = QH // KVH
GROUP = PER * HD
KV = KVH * HD
STACK = PER * SEQ
BLK = 256
LAYERS, NX, NY, NZ = 8, 4, 4, 8
EPSILON = 1e-05
NT = (((1,), (1,)), ((), ()))


def mod(a, n):
    return lax.rem(a + 2 * n, n)


def aligned(index, size):
    return pl.multiple_of(index * size, size)


def body(
    x_hbm, q_hbm, k_ref, gain_ref, w_hbm, og_hbm, out_ref,
    xv, qv, wall, xi, pt, inv_in, gain_in, p_own, inv_own, mask, top, up, vgb, vr,
    h_own, h_all, vg_all, vg_t, rs_send, rs_recv, total, n_own, n1, n2, n3,
    s_loc, s_x, r_x, s_p, r_p, s_i, r_i, s_g, r_g, s_og, r_og, s_wx, r_w, s_z, s_y, s_yf, r_y,
    s_pt, r_pt, s_v, r_v, s_vg, r_vg, s_vp, r_vp, s_vy, r_vy, s_h, r_h, s_rs, r_rs, s_n, r_n,
):
    sec, dp = lax.axis_index("section"), lax.axis_index("dp")
    x, c = lax.div(sec, 2), lax.rem(sec, 2)
    z, y = lax.div(dp, NY), lax.rem(dp, NY)
    mate = sec + 1 - 2 * c

    def at_dp(zz, yy):
        return zz * NY + yy

    def send(src, dst, ssem, rsem, section=sec, replica=dp):
        return pltpu.make_async_remote_copy(
            src_ref=src, dst_ref=dst, send_sem=ssem, recv_sem=rsem,
            device_id={"section": section, "dp": replica}, device_id_type=MESH,
        )

    def arrived(dst, rsem):
        send(dst, dst, s_loc.at[7], rsem, section=mate).wait_recv()

    pending = []

    def go(copy, when=None):
        if when is None:
            copy.start()
        else:
            pl.when(when)(copy.start)
        pending.append((copy, when))

    barrier = pltpu.get_barrier_semaphore()
    friends = [(mod(sec + k, LAYERS), dp) for k in range(1, LAYERS)]
    friends += [(sec, at_dp(z, mod(y + k, NY))) for k in range(1, NY)]
    friends += [(sec, at_dp(mod(z + k, NZ), y)) for k in range(1, NZ)]
    for section, replica in friends:
        pl.semaphore_signal(
            barrier, inc=1, device_id={"section": section, "dp": replica}, device_id_type=MESH
        )
    pl.semaphore_wait(barrier, len(friends))

    w_home = lax.div(z, 2)
    w_zl = lax.rem(z, 2)
    w_away = w_home != x
    go(
        send(
            w_hbm, wall.at[c, x, w_zl * NY + y], s_wx, r_w.at[x, w_zl], section=2 * w_home + c
        ),
        w_away,
    )
    w_local = pltpu.make_async_copy(w_hbm, wall.at[c, x, w_zl * NY + y], s_loc.at[0])
    pl.when(jnp.logical_not(w_away))(w_local.start)
    x_load = pltpu.make_async_copy(x_hbm, xv, s_loc.at[1])
    q_load = pltpu.make_async_copy(q_hbm, qv, s_loc.at[2])
    q_load.start()
    x_load.start()

    def rows(b):
        return pl.ds(pl.multiple_of(b * SEQ, 16), SEQ)

    half = D // LAYERS
    go(
        send(
            og_hbm.at[rows(1 - c)], top.at[:, pl.ds(aligned(c, half), half)], s_og, r_og,
            section=mate,
        )
    )
    og_local = pltpu.make_async_copy(
        og_hbm.at[rows(c)], top.at[:, pl.ds(aligned(c, half), half)], s_loc.at[3]
    )
    og_local.start()

    def dest(k):
        section = mod(sec + k, LAYERS)
        return section, lax.div(section, 2), lax.rem(section, 2)

    def block(ref, b, g):
        return ref.at[rows(b), pl.ds(aligned(g, GROUP), GROUP)]

    for k in range(1, LAYERS):
        section, g, b = dest(k)
        go(send(block(x_hbm, b, g), xi.at[sec], s_x.at[k], r_x.at[sec], section=section))
        go(
            send(
                gain_ref.at[:, pl.ds(aligned(g, GROUP), GROUP)], gain_in.at[sec], s_g.at[k],
                r_g.at[sec], section=section,
            )
        )
    xi_local = pltpu.make_async_copy(block(x_hbm, c, x), xi.at[sec], s_loc.at[4])
    xi_local.start()
    gain_in[sec] = gain_ref[:, pl.ds(aligned(x, GROUP), GROUP)]

    key_row = lax.broadcasted_iota(jnp.int32, (SEQ, STACK), 0)
    query_row = lax.rem(lax.broadcasted_iota(jnp.int32, (SEQ, STACK), 1), SEQ)
    mask[...] = jnp.where(key_row <= query_row, 0.0, -1e30).astype(F32)
    q_load.wait()

    def probabilities(g, b):
        keys = k_ref[rows(b), pl.ds(aligned(g, HD), HD)]
        stacked = jnp.concatenate(
            [
                qv[rows(b), pl.ds(pl.multiple_of(g * GROUP + h * HD, HD), HD)]
                for h in range(PER)
            ],
            axis=0,
        )
        scores = lax.dot_general(keys, stacked, NT, preferred_element_type=F32)
        scores = scores * HD ** (-0.5) + mask[...]
        exponent = jnp.exp(scores - jnp.max(scores, axis=0, keepdims=True))
        return (exponent / jnp.sum(exponent, axis=0, keepdims=True)).astype(BF16)

    def p_copy(k):
        section, g, b = dest(k)
        return send(p_own.at[k], pt.at[sec], s_p.at[k], r_p.at[sec], section=section)

    @pl.loop(1, LAYERS)
    def _(k):
        section, g, b = dest(k)
        p_own[k] = probabilities(g, b)
        p_copy(k).start()

    pt[sec] = probabilities(x, c)

    x_load.wait()

    def squares(i, acc):
        v = xv[:, pl.ds(aligned(i, HD), HD)].astype(F32)
        return acc + v * v

    acc = lax.fori_loop(0, D // HD, squares, jnp.zeros((2 * SEQ, HD), F32))
    mean = jnp.sum(acc, axis=1, keepdims=True) * (1.0 / D)
    inv_own[...] = jnp.broadcast_to(lax.rsqrt(mean + EPSILON), (2 * SEQ, HD))
    for k in range(1, LAYERS):
        section, g, b = dest(k)
        go(send(inv_own.at[rows(b)], inv_in.at[sec], s_i.at[k], r_i.at[sec], section=section))
    inv_in[sec] = inv_own[rows(c)]

    @pl.loop(0, D // BLK)
    def _(i):
        cols = pl.ds(aligned(i, BLK), BLK)
        normed = xv[:, cols].astype(F32) * inv_own[:, 0:1]
        h_own[lax.rem(i, NY), :, pl.ds(aligned(lax.div(i, NY), BLK), BLK)] = (
            normed * gain_ref[0:1, cols]
        ).astype(BF16)

    d = mod(2 * x - z, NZ)
    downward = d <= 3
    step = jnp.where(downward, -1, 1)
    first = jnp.where(downward, 0, 1)
    source = jnp.logical_or(d == 0, d == 7)
    onward = jnp.logical_and(d != 3, d != 4)
    z_out, z_in = mod(z + step, NZ), mod(z - step, NZ)
    y_right, y_left, y_far = mod(y + 1, NY), mod(y - 1, NY), mod(y + 2, NY)

    def piece_ref(u, piece, yy):
        return wall.at[c, u, piece * NY + yy]

    def column(u):
        for o in range(2):
            piece = first if o == 0 else 1 - first
            ref = piece_ref(u, piece, y)
            sem = r_w.at[u, piece]
            if o == 0:
                mine = jnp.logical_and(source, x == u)
                pl.when(mine)(w_local.wait)
                pl.when(jnp.logical_not(mine))(lambda ref=ref, sem=sem: arrived(ref, sem))
                go(send(ref, ref, s_z.at[u, 2], sem, replica=at_dp(z_in, y)), source)
            else:
                arrived(ref, sem)
            go(send(ref, ref, s_z.at[u, o], sem, replica=at_dp(z_out, y)), onward)
            for i, yy in enumerate((y_right, y_left)):
                go(send(ref, ref, s_y.at[u, o, i], r_y.at[u, piece, y], replica=at_dp(z, yy)))

    def row(u):
        def near(piece, yy):
            arrived(piece_ref(u, piece, yy), r_y.at[u, piece, yy])

        def forward(piece, source_y, to_y, i):
            ref = piece_ref(u, piece, source_y)
            go(send(ref, ref, s_yf.at[u, i], r_y.at[u, piece, source_y], replica=at_dp(z, to_y)))

        near(0, y_left)
        forward(0, y_left, y_right, 0)
        near(1, y_right)
        forward(1, y_right, y_left, 1)
        near(1, y_left)
        near(0, y_right)

    def finish(u):
        for piece in range(2):
            arrived(piece_ref(u, piece, y_far), r_y.at[u, piece, y_far])
        go(send(wall.at[c, u], wall.at[c, u], s_pt.at[u], r_pt.at[u], section=mate))

    def weights_ready(u):
        arrived(wall.at[1 - c, u], r_pt.at[u])

    column(3)
    column(2)
    row(3)
    column(1)
    row(2)
    finish(3)
    column(0)
    row(1)
    finish(2)
    row(0)
    finish(1)
    finish(0)

    for k in range(1, NY):
        yy = mod(y + k, NY)
        mine = h_all.at[pl.ds(aligned(y, 2 * SEQ), 2 * SEQ)]
        go(send(h_own.at[yy], mine, s_h.at[k], r_h.at[y], replica=at_dp(z, yy)))
    h_all[pl.ds(aligned(y, 2 * SEQ), 2 * SEQ), :] = h_own[y]

    og_local.wait()
    arrived(top.at[:, pl.ds(aligned(1 - c, half), half)], r_og)
    for h in range(PER):
        up[h * SEQ:(h + 1) * SEQ, :] = top[:, h * HD:(h + 1) * HD]
    xi_local.wait()
    for u in range(NX):
        weights_ready(u)
    for k in range(1, LAYERS):
        section = mod(sec + k, LAYERS)
        arrived(xi.at[section], r_x.at[section])
        arrived(pt.at[section], r_p.at[section])
        arrived(inv_in.at[section], r_i.at[section])
        arrived(gain_in.at[section], r_g.at[section])

    def peers():
        return [mod(x + k, NX) for k in range(1, NX)]

    def w_block(s, i):
        return wall[lax.rem(s, 2), lax.div(s, 2), i]

    def v_copies(s):
        return [
            send(vr.at[s, x], vr.at[s, x], s_v.at[s, k], r_v.at[s, x], section=2 * g + c)
            for k, g in enumerate(peers())
        ]

    def projected(s):
        inverse = inv_in[s][:, 0:1]
        acc = jnp.zeros((SEQ, KV), F32)
        for i in range(GROUP // BLK):
            cols = slice(i * BLK, (i + 1) * BLK)
            normed = xi[s, :, cols].astype(F32) * inverse
            hidden = (normed * gain_in[s, 0:1, cols]).astype(BF16)
            acc += jnp.dot(hidden, w_block(s, i), preferred_element_type=F32)
        vr[s, x] = acc.astype(BF16)
        for copy in v_copies(s):
            copy.start()

    @pl.loop(0, LAYERS)
    def _(t):
        projected(LAYERS - 1 - t)

    def vg_cols(s, g):
        return vgb.at[s, :, pl.ds(aligned(g, HD), HD)]

    def vg_copies(s):
        return [
            send(vg_cols(s, x), vg_cols(s, x), s_vg.at[s, k], r_vg.at[s, x], section=2 * g + c)
            for k, g in enumerate(peers())
        ]

    def vp_copy(s):
        place = vg_all.at[pl.ds(pl.multiple_of(y * 2 * SEQ + c * SEQ, 16), SEQ)]
        return send(vgb.at[s], place, s_vp, r_vp, section=mate)

    def value_grad(s):
        grad = jnp.dot(pt[s], up[...], preferred_element_type=F32).astype(BF16)
        vgb[s, :, pl.ds(aligned(x, HD), HD)] = grad
        for copy in vg_copies(s):
            copy.start()
        for g in peers():
            arrived(vr.at[s, g], r_v.at[s, g])
        for g in peers():
            arrived(vg_cols(s, g), r_vg.at[s, g])
        pl.when(s == mate)(lambda: vp_copy(s).start())

    def layer(s):
        value_grad(s)
        grads = vgb[s]
        inner = sum(vr[s, g].astype(F32) for g in range(NX))
        inner = jnp.sum(grads.astype(F32) * inner, axis=1, keepdims=True) * (1.0 / D)
        inverse = inv_in[s][:, 0:1]
        for i in range(GROUP // BLK):
            cols = slice(i * BLK, (i + 1) * BLK)
            hidden_grad = lax.dot_general(grads, w_block(s, i), NT, preferred_element_type=F32)
            normed = xi[s, :, cols].astype(F32) * inverse
            change = inverse * (hidden_grad * gain_in[s, 0:1, cols] - normed * inner)
            for j in range(BLK // HD):
                h = i * (BLK // HD) + j
                place = slice(h * SEQ, (h + 1) * SEQ)
                up[place, :] = (
                    up[place, :].astype(F32) + change[:, j * HD:(j + 1) * HD]
                ).astype(BF16)

    @pl.loop(0, LAYERS - 1)
    def _(t):
        layer(LAYERS - 1 - t)

    value_grad(0)

    vg_all[pl.ds(pl.multiple_of(y * 2 * SEQ + c * SEQ, 16), SEQ)] = vgb[sec]
    arrived(vg_all.at[pl.ds(pl.multiple_of(y * 2 * SEQ + (1 - c) * SEQ, 16), SEQ)], r_vp)

    def vg_rows(yy):
        return vg_all.at[pl.ds(aligned(yy, 2 * SEQ), 2 * SEQ)]

    for k in range(1, NY):
        yy = mod(y + k, NY)
        go(send(vg_rows(y), vg_rows(y), s_vy.at[k], r_vy.at[y], replica=at_dp(z, yy)))
    for k in range(1, NY):
        yy = mod(y + k, NY)
        arrived(h_all.at[pl.ds(aligned(yy, 2 * SEQ), 2 * SEQ)], r_h.at[yy])
    for k in range(1, NY):
        yy = mod(y + k, NY)
        arrived(vg_rows(yy), r_vy.at[yy])
    vg_t[...] = vg_all[...].astype(F32).T.astype(BF16)

    def product(way, owner):
        return jnp.dot(
            vg_t[way * BLK:(way + 1) * BLK, :], h_all[:, pl.ds(aligned(owner, BLK), BLK)],
            preferred_element_type=F32,
        )

    def rs_copy(way, k):
        zz = mod(z + 1, NZ) if way == 0 else mod(z - 1, NZ)
        return send(
            rs_send.at[way, k], rs_recv.at[way, k], s_rs.at[way, k], r_rs.at[way, k],
            replica=at_dp(zz, y),
        )

    def owner_at(way, k):
        return mod(z - 1 - k, NZ) if way == 0 else mod(z + 1 + k, NZ)

    for way in range(2):
        rs_send[way, 0] = product(way, owner_at(way, 0)).astype(BF16)
        rs_copy(way, 0).start()

    @pl.loop(1, NZ - 1)
    def _(k):
        for way in range(2):
            total[way] = product(way, owner_at(way, k))
        for way in range(2):
            rs_copy(way, k - 1).wait_recv()
            rs_send[way, k] = (total[way] + rs_recv[way, k - 1].astype(F32)).astype(BF16)
            rs_copy(way, k).start()

    squares_sum = jnp.zeros((1, 1), F32)
    for way in range(2):
        total[way] = product(way, z)
    for way in range(2):
        rs_copy(way, NZ - 2).wait_recv()
        owned = total[way] + rs_recv[way, NZ - 2].astype(F32)
        total[way] = owned
        part = jnp.sum(owned * owned, axis=1, keepdims=True)
        squares_sum += jnp.sum(part, axis=0, keepdims=True)

    stages = (
        (n1, LAYERS, sec, lambda i: (i, dp)),
        (n2, NY, y, lambda i: (sec, at_dp(z, i))),
        (n3, NZ, z, lambda i: (sec, at_dp(i, y))),
    )
    value = jnp.broadcast_to(squares_sum, (8, 128))
    for t, (slots, count, me, place) in enumerate(stages):
        slots[me] = value
        for k in range(1, count):
            section, replica = place(mod(me + k, count))
            go(
                send(
                    slots.at[me], slots.at[me], s_n.at[t, k], r_n.at[t, me], section=section,
                    replica=replica,
                )
            )
        for k in range(1, count):
            i = mod(me + k, count)
            arrived(slots.at[i], r_n.at[t, i])
        value = sum(slots[i] for i in range(count))
    ceiling = float(LAYERS * D * KV) ** 0.5
    factor = jnp.minimum(1.0, ceiling / jnp.sqrt(value[0:1, 0:1]))
    for way in range(2):
        out_ref[:, way * BLK:(way + 1) * BLK] = (total[way] * factor).T

    @pl.loop(1, LAYERS)
    def _(k):
        p_copy(k).wait_send()

    @pl.loop(0, LAYERS)
    def _(s):
        for copy in v_copies(s) + vg_copies(s):
            copy.wait_send()

    vp_copy(mate).wait_send()

    @pl.loop(0, NZ - 1)
    def _(k):
        for way in range(2):
            rs_copy(way, k).wait_send()

    for copy, when in pending:
        if when is None:
            copy.wait_send()
        else:
            pl.when(when)(copy.wait_send)


def shards(layer_inputs, queries, keys, gains, value_weights, out_grad):
    gain_rows = jnp.broadcast_to(gains.astype(F32), (8, D))
    dma, vmem = pltpu.SemaphoreType.DMA, pltpu.VMEM
    scratch = [
        vmem((2 * SEQ, D), BF16),
        vmem((2 * SEQ, D), BF16),
        vmem((2, NX, 2 * NY, BLK, KV), BF16),
        vmem((LAYERS, SEQ, GROUP), BF16),
        vmem((LAYERS, SEQ, STACK), BF16),
        vmem((LAYERS, SEQ, HD), F32),
        vmem((LAYERS, 8, GROUP), F32),
        vmem((LAYERS, SEQ, STACK), BF16),
        vmem((2 * SEQ, HD), F32),
        vmem((SEQ, STACK), F32),
        vmem((SEQ, GROUP), BF16),
        vmem((STACK, HD), BF16),
        vmem((LAYERS, SEQ, KV), BF16),
        vmem((LAYERS, NX, SEQ, KV), BF16),
        vmem((NY, 2 * SEQ, GROUP), BF16),
        vmem((NY * 2 * SEQ, GROUP), BF16),
        vmem((NY * 2 * SEQ, KV), BF16),
        vmem((KV, NY * 2 * SEQ), BF16),
        vmem((2, NZ - 1, BLK, BLK), BF16),
        vmem((2, NZ - 1, BLK, BLK), BF16),
        vmem((2, BLK, BLK), F32),
        vmem((8, 128), F32),
        vmem((LAYERS, 8, 128), F32),
        vmem((NY, 8, 128), F32),
        vmem((NZ, 8, 128), F32),
        dma((8,)),
        dma((LAYERS,)), dma((LAYERS,)),
        dma((LAYERS,)), dma((LAYERS,)),
        dma((LAYERS,)), dma((LAYERS,)),
        dma((LAYERS,)), dma((LAYERS,)),
        dma, dma,
        dma, dma((NX, 2)), dma((NX, 3)), dma((NX, 2, 2)), dma((NX, 2)), dma((NX, 2, NY)),
        dma((NX,)), dma((NX,)),
        dma((LAYERS, NX)), dma((LAYERS, NX)),
        dma((LAYERS, NX)), dma((LAYERS, NX)),
        dma, dma,
        dma((NY,)), dma((NY,)),
        dma((NY,)), dma((NY,)),
        dma((2, NZ)), dma((2, NZ)),
        dma((3, LAYERS)), dma((3, LAYERS)),
    ]
    hbm, whole = pl.BlockSpec(memory_space=pl.ANY), pl.BlockSpec(memory_space=pltpu.VMEM)
    out = pl.pallas_call(
        body,
        out_shape=jax.ShapeDtypeStruct((BLK, KV), F32),
        in_specs=[hbm, hbm, whole, whole, hbm, hbm],
        out_specs=whole,
        scratch_shapes=scratch,
        compiler_params=pltpu.CompilerParams(
            collective_id=0, has_side_effects=True, vmem_limit_bytes=60 * 1024 * 1024
        ),
    )(layer_inputs[0], queries[0], keys[0], gain_rows, value_weights[0], out_grad)
    return out[None]


def solution(mesh):
    return jax.shard_map(
        shards,
        mesh=mesh,
        in_specs=(
            P("section", "dp", None),
            P("section", "dp", None),
            P("section", "dp", None),
            P("section", None),
            P("section", "dp", None),
            P("dp", "section"),
        ),
        out_specs=P("section", "dp", None),
        check_vma=False,
    )
```

time: 811 us -> 249 us (0.31)
  waiting for transfers between devices: 415 us -> 0 us
  Pallas kernels: 0 us -> 246 us
  other arithmetic: 180 us -> 0.79 us
  blocking collectives: 78.4 us -> 0 us
  local copies, waits for them, and re-layouts: 74.8 us -> 2.59 us
  matrix products: 26.6 us -> 0 us
  starting transfers between devices: 21.1 us -> 0 us
  between operations: 13.8 us -> 0.01 us
    pallas_call x0 -> x1, Pallas kernels: none -> 246 us  [shards(): pl.pallas_call(body, out_shape=jax.ShapeDtypeStruct((BLK, KV), F32), in_s...]
    reduce_scatter x1 -> x0, waiting for transfers between devices: 220 us -> none  [shards(): lax.psum_scatter(running.astype(jnp.bfloat16), 'dp', scatter_dimension=0,...]
    add x9 -> x0, other arithmetic: 153 us -> none  [turn(): return (incoming, grad_rows, hidden_rows, running + partial_value)]
    all_gather x2 -> x0, waiting for transfers between devices: 134 us -> none  [the longest x1 101 us: shards(): weights = lax.all_gather(value_weights[0], 'dp', axis=0, tiled=True)]
    psum x1 -> x0, blocking collectives: 78.4 us -> none  [shards(): square_sum = lax.psum(jnp.sum(owned_rows * owned_rows), ('section', 'dp'))]
    another operation x19 -> x0, local copies, waits for them, and re-layouts: 69.1 us -> none
    ppermute x9 -> x0, waiting for transfers between devices: 59.8 us -> none  [passed_along(): return lax.ppermute(block, axis, route)]
    dot_general x8 -> x0, matrix products: 26.6 us -> none  [the longest x2 16.4 us: run_block(): jnp.einsum('td,tk->dk', hidden, value_grad, preferred_element_type=jnp.fl...]
  transfers between devices with their start and end apart: 12 -> 0, of which waited for: 5 -> 0; matrix products, arithmetic and copies ran while one was open for 19% -> 0% of each run, Pallas kernels for 0% -> 0%
where the time goes in v1:
time: 249 us
  Pallas kernels  246 us (99%)
  local copies, waits for them, and re-layouts  2.59 us (1%)
    pallas_call x1, Pallas kernels, shards(): pl.pallas_call(body, out_shape=jax.ShapeDtypeStruct((BLK, KV), F32), in_s...  246 us

profile of v1, /device:TPU:1, one launch (start us, length us, event | category | flops | bytes accessed | tf_op | source)
XLA Modules:
  0.0 249.3 jit_solution(12183335298065534618)
XLA Ops:
  0.0 0.8 broadcast_in_dim.17
  0.8 0.7 broadcast_in_dim.15.gain_ref
  1.5 245.9 %shard_map.64 = f32[256,512]{1,0:T(8,128)} custom-call(bf16[160,8192]{1,0:T(8,128)(2,1)} %bitcast.6, bf16[160,8192]{1,0:T(8,128)(2,1)} %bitcast.7, bf16[160,512]{1,0:T(8,128)(2,1)} %bitcast.10, f32[8,8192]{1,0:T(8,128)} %broadcast_in_dim.15.gain_ref, bf16[256,512]{1,0:T(8,128)(2,1)} %bitcast.9, bf16[160,1024]{1,0:T(8,128)(2,1)} %og_hbm.1), custom_call_target="tpu_custom_call" | custom-call | tf_op jit(solution)/shard_map/pallas_call | solution.py:486
  247.4 1.9 copy.8

commit v2 on v1

v2 whole, which is shorter than its diff:
```python
import jax
import jax.numpy as jnp
from jax import lax
from jax.experimental import pallas as pl
from jax.experimental.pallas import tpu as pltpu
from jax.sharding import PartitionSpec as P

MESH = pl.DeviceIdType.MESH
F32, BF16 = jnp.float32, jnp.bfloat16
QH, KVH, HD, SEQ, D = 64, 4, 128, 80, 8192
PER = QH // KVH
GROUP = PER * HD
KV = KVH * HD
STACK = PER * SEQ
BLK = 256
CUT = 128
HOPS = 4
STREAMS = KV // CUT
LAYERS, NX, NY, NZ = 8, 4, 4, 8
EPSILON = 1e-05
NT = (((1,), (1,)), ((), ()))


def mod(a, n):
    return lax.rem(a + 2 * n, n)


def aligned(index, size):
    return pl.multiple_of(index * size, size)


def body(
    x_hbm, q_hbm, k_ref, gain_bf, w_hbm, og_hbm, out_ref, gain_ref,
    xv, qv, wall, xi, pt, inv_in, gain_in, p_own, inv_own, mask, top, up, vgb, v_own, v_in, v_all, hg, inner_in,
    h_own, h_all, vg_all, vg_t, rs_send, rs_recv, total, n1, n2, n3,
    s_loc, s_x, r_x, s_p, r_p, s_i, r_i, s_g, r_g, s_og, r_og, s_wx, r_w, s_z, s_y, s_yf, r_y,
    s_pt, r_pt, s_v, r_v, s_w, r_vs, s_in, r_in, s_vg, r_vg, s_vp, r_vp, s_vy, r_vy, s_h, r_h, s_rs, r_rs, s_n, r_n,
):
    sec, dp = lax.axis_index("section"), lax.axis_index("dp")
    x, c = lax.div(sec, 2), lax.rem(sec, 2)
    z, y = lax.div(dp, NY), lax.rem(dp, NY)
    mate = sec + 1 - 2 * c

    def at_dp(zz, yy):
        return zz * NY + yy

    def send(src, dst, ssem, rsem, section=sec, replica=dp):
        return pltpu.make_async_remote_copy(
            src_ref=src, dst_ref=dst, send_sem=ssem, recv_sem=rsem,
            device_id={"section": section, "dp": replica}, device_id_type=MESH,
        )

    def arrived(dst, rsem):
        send(dst, dst, s_loc.at[7], rsem, section=mate).wait_recv()

    pending, drains = [], []

    def go(copy, when=None):
        if when is None:
            copy.start()
        else:
            pl.when(when)(copy.start)
        pending.append((copy, when))

    barrier = pltpu.get_barrier_semaphore()
    friends = [(mod(sec + k, LAYERS), dp) for k in range(1, LAYERS)]
    friends += [(sec, at_dp(z, mod(y + k, NY))) for k in range(1, NY)]
    friends += [(sec, at_dp(mod(z + k, NZ), y)) for k in range(1, NZ)]
    for section, replica in friends:
        pl.semaphore_signal(
            barrier, inc=1, device_id={"section": section, "dp": replica}, device_id_type=MESH
        )
    pl.semaphore_wait(barrier, len(friends))

    w_home = lax.div(z, 2)
    w_zl = lax.rem(z, 2)
    w_away = w_home != x
    w_place = wall.at[c, x, w_zl * NY + y]
    w_local = pltpu.make_async_copy(w_hbm, w_place, s_loc.at[0])
    x_load = pltpu.make_async_copy(x_hbm, xv, s_loc.at[1])
    q_load = pltpu.make_async_copy(q_hbm, qv, s_loc.at[2])
    half = D // LAYERS

    def rows(b):
        return pl.ds(pl.multiple_of(b * SEQ, 16), SEQ)

    def top_half(b):
        return top.at[:, pl.ds(aligned(b, half), half)]

    og_local = pltpu.make_async_copy(og_hbm.at[rows(c)], top_half(c), s_loc.at[3])

    def dest(k):
        section = mod(sec + k, LAYERS)
        return section, lax.div(section, 2), lax.rem(section, 2)

    def block(ref, b, g):
        return ref.at[rows(b), pl.ds(aligned(g, GROUP), GROUP)]

    xi_local = pltpu.make_async_copy(block(x_hbm, c, x), xi.at[sec], s_loc.at[4])

    def send_weights():
        used = sec != 0
        for h in range(2):
            part = pl.ds(h * CUT, CUT)
            go(
                send(
                    w_hbm.at[part], w_place.at[part], s_wx.at[h], r_w.at[x, w_zl, h],
                    section=2 * w_home + c,
                ),
                jnp.logical_and(used, w_away),
            )
        pl.when(jnp.logical_and(used, jnp.logical_not(w_away)))(w_local.start)

    def send_inputs():
        for i in range(D // BLK):
            gain_ref[i:i + 1, :] = gain_bf[:, i * BLK:(i + 1) * BLK].astype(F32)
        q_load.start()
        x_load.start()
        go(send(og_hbm.at[rows(1 - c)], top_half(c), s_og, r_og, section=mate))
        og_local.start()
        for k in range(1, LAYERS):
            section, g, b = dest(k)
            go(send(block(x_hbm, b, g), xi.at[sec], s_x.at[k], r_x.at[sec], section=section))
            gain = gain_ref.at[pl.ds(aligned(g, 8), 8)]
            go(send(gain, gain_in.at[sec], s_g.at[k], r_g.at[sec], section=section))
        xi_local.start()
        gain_in[sec] = gain_ref[pl.ds(aligned(x, 8), 8)]

    def probabilities(g, b):
        keys = k_ref[rows(b), pl.ds(aligned(g, HD), HD)]
        stacked = jnp.concatenate(
            [
                qv[rows(b), pl.ds(pl.multiple_of(g * GROUP + h * HD, HD), HD)]
                for h in range(PER)
            ],
            axis=0,
        )
        scores = lax.dot_general(keys, stacked, NT, preferred_element_type=F32)
        scores = scores * HD ** (-0.5) + mask[...]
        exponent = jnp.exp(scores - jnp.max(scores, axis=0, keepdims=True))
        return (exponent / jnp.sum(exponent, axis=0, keepdims=True)).astype(BF16)

    def p_copy(k):
        section, g, b = dest(k)
        return send(p_own.at[k], pt.at[sec], s_p.at[k], r_p.at[sec], section=section)

    def send_probabilities():
        key_row = lax.broadcasted_iota(jnp.int32, (SEQ, STACK), 0)
        query_row = lax.rem(lax.broadcasted_iota(jnp.int32, (SEQ, STACK), 1), SEQ)
        mask[...] = jnp.where(key_row <= query_row, 0.0, -1e30).astype(F32)
        q_load.wait()

        @pl.loop(1, LAYERS)
        def _(k):
            section, g, b = dest(k)
            p_own[k] = probabilities(g, b)
            p_copy(k).start()

        pt[sec] = probabilities(x, c)

        def drain():
            @pl.loop(1, LAYERS)
            def _(k):
                p_copy(k).wait_send()

        drains.append(drain)

    def send_inverse():
        x_load.wait()

        def squares(i, acc):
            v = xv[:, pl.ds(aligned(i, HD), HD)].astype(F32)
            return acc + v * v

        acc = lax.fori_loop(0, D // HD, squares, jnp.zeros((2 * SEQ, HD), F32))
        mean = jnp.sum(acc, axis=1, keepdims=True) * (1.0 / D)
        inv_own[...] = jnp.broadcast_to(lax.rsqrt(mean + EPSILON), (2 * SEQ, HD))
        for k in range(1, LAYERS):
            section, g, b = dest(k)
            go(send(inv_own.at[rows(b)], inv_in.at[sec], s_i.at[k], r_i.at[sec], section=section))
        inv_in[sec] = inv_own[rows(c)]

    def make_hidden():
        @pl.loop(0, D // BLK)
        def _(i):
            cols = pl.ds(aligned(i, BLK), BLK)
            normed = xv[:, cols].astype(F32) * inv_own[:, 0:1]
            h_own[lax.rem(i, NY), :, pl.ds(aligned(lax.div(i, NY), BLK), BLK)] = (
                normed * gain_ref[pl.ds(i, 1), :]
            ).astype(BF16)

    d = mod(2 * x - z, NZ)
    downward = d <= 3
    step = jnp.where(downward, -1, 1)
    first = jnp.where(downward, 0, 1)
    source = jnp.logical_or(d == 0, d == 7)
    onward = jnp.logical_and(d != 3, d != 4)
    z_out, z_in = mod(z + step, NZ), mod(z - step, NZ)
    y_right, y_left, y_far = mod(y + 1, NY), mod(y - 1, NY), mod(y + 2, NY)

    def piece_ref(u, piece, yy, h):
        return wall.at[c, u, piece * NY + yy, pl.ds(h * CUT, CUT)]

    def live(u, cond=None):
        if u > 0:
            return cond
        return c == 1 if cond is None else jnp.logical_and(c == 1, cond)

    def arrived_if(cond, dst, rsem):
        if cond is None:
            arrived(dst, rsem)
        else:
            pl.when(cond)(lambda: arrived(dst, rsem))

    def column(u):
        for o in range(2):
            piece = first if o == 0 else 1 - first
            if o == 0:
                mine = jnp.logical_and(source, x == u)
                pl.when(live(u, mine))(w_local.wait)
            for h in range(2):
                ref = piece_ref(u, piece, y, h)
                sem = r_w.at[u, piece, h]
                if o == 0:
                    arrived_if(live(u, jnp.logical_not(mine)), ref, sem)
                    inward = send(ref, ref, s_z.at[u, 2, h], sem, replica=at_dp(z_in, y))
                    go(inward, live(u, source))
                else:
                    arrived_if(live(u), ref, sem)
                outward = send(ref, ref, s_z.at[u, o, h], sem, replica=at_dp(z_out, y))
                go(outward, live(u, onward))
                for i, yy in enumerate((y_right, y_left)):
                    sems = s_y.at[u, o, i, h], r_y.at[u, piece, y, h]
                    go(send(ref, ref, *sems, replica=at_dp(z, yy)), live(u))

    def near(u, piece, yy, h):
        arrived_if(live(u), piece_ref(u, piece, yy, h), r_y.at[u, piece, yy, h])

    def row(u):
        for h in range(2):
            for piece, source_y, to_y in ((0, y_left, y_right), (1, y_right, y_left)):
                near(u, piece, source_y, h)
                ref = piece_ref(u, piece, source_y, h)
                sems = s_yf.at[u, piece, h], r_y.at[u, piece, source_y, h]
                go(send(ref, ref, *sems, replica=at_dp(z, to_y)), live(u))

    def finish(u):
        for h in range(2):
            near(u, 1, y_left, h)
            near(u, 0, y_right, h)
        for h in range(2):
            for piece in range(2):
                near(u, piece, y_far, h)
        go(send(wall.at[c, u], wall.at[c, u], s_pt.at[u], r_pt.at[u], section=mate), live(u))

    def weights_ready(u):
        cond = None if u > 0 else c == 0
        arrived_if(cond, wall.at[1 - c, u], r_pt.at[u])

    def h_rows(yy):
        return h_all.at[pl.ds(aligned(yy, 2 * SEQ), 2 * SEQ)]

    def send_hidden():
        for k in range(1, NY):
            yy = mod(y + k, NY)
            go(send(h_own.at[yy], h_rows(y), s_h.at[k], r_h.at[y], replica=at_dp(z, yy)))
        h_all[pl.ds(aligned(y, 2 * SEQ), 2 * SEQ), :] = h_own[y]

    def hidden_ready():
        for k in range(1, NY):
            yy = mod(y + k, NY)
            arrived(h_rows(yy), r_h.at[yy])

    def top_ready():
        og_local.wait()
        arrived(top_half(1 - c), r_og)
        for h in range(PER):
            up[h * SEQ:(h + 1) * SEQ, :] = top[:, h * HD:(h + 1) * HD]

    def inputs_ready(s):
        pl.when(s == sec)(xi_local.wait)

        @pl.when(s != sec)
        def _():
            arrived(xi.at[s], r_x.at[s])
            arrived(pt.at[s], r_p.at[s])
            arrived(inv_in.at[s], r_i.at[s])
            arrived(gain_in.at[s], r_g.at[s])

    def peers():
        return [mod(x + k, NX) for k in range(1, NX)]

    def w_block(s, i):
        return wall[s % 2, s // 2, i]

    def v_part(s, k):
        g = mod(x + k, NX)
        return send(
            v_own.at[s, g], v_in.at[s, x], s_v.at[s, k], r_v.at[s, x], section=2 * g + c
        )

    def v_start(s):
        inverse = inv_in[s][:, 0:1]
        acc = jnp.zeros((SEQ, KV), F32)
        for i in range(GROUP // BLK):
            cols = slice(i * BLK, (i + 1) * BLK)
            normed = xi[s, :, cols].astype(F32) * inverse
            hidden = (normed * gain_in[s, i:i + 1, :]).astype(BF16)
            acc += jnp.dot(hidden, w_block(s, i), preferred_element_type=F32)
        for g in range(NX):
            v_own[s, g] = acc[:, g * HD:(g + 1) * HD].astype(BF16)
        for k in range(1, NX):
            v_part(s, k).start()

    def v_cols(s, g):
        return v_all.at[s, :, pl.ds(aligned(g, HD), HD)]

    def v_sum_copy(s, k):
        g = mod(x + k, NX)
        return send(v_cols(s, x), v_cols(s, x), s_w.at[s, k], r_vs.at[s, x], section=2 * g + c)

    def v_sum(s):
        acc = v_own[s, x].astype(F32)
        for g in peers():
            arrived(v_in.at[s, g], r_v.at[s, g])
            acc += v_in[s, g].astype(F32)
        v_all[s, :, pl.ds(aligned(x, HD), HD)] = acc.astype(BF16)
        for k in range(1, NX):
            v_sum_copy(s, k).start()

    def v_ready(s):
        for g in peers():
            arrived(v_cols(s, g), r_vs.at[s, g])

    def vg_cols(s, g):
        return vgb.at[s, :, pl.ds(aligned(g, HD), HD)]

    def vg_copies(s):
        return [
            send(vg_cols(s, x), vg_cols(s, x), s_vg.at[s, k], r_vg.at[s, x], section=2 * g + c)
            for k, g in enumerate(peers())
        ]

    def vg_place(b):
        return pl.ds(pl.multiple_of(y * 2 * SEQ + b * SEQ, 16), SEQ)

    def vp_copy(s):
        return send(vgb.at[s], vg_all.at[vg_place(c)], s_vp, r_vp, section=mate)

    def vg_start(s):
        grad = jnp.dot(pt[s], up[...], preferred_element_type=F32).astype(BF16)
        vgb[s, :, pl.ds(aligned(x, HD), HD)] = grad
        for copy in vg_copies(s):
            copy.start()

    def vg_ready(s):
        for g in peers():
            arrived(vg_cols(s, g), r_vg.at[s, g])
        pl.when(mate == s)(lambda: vp_copy(s).start())

    def update(s):
        grads = vgb[s]
        inner = grads.astype(F32) * v_all[s].astype(F32)
        inner = jnp.sum(inner, axis=1, keepdims=True) * (1.0 / D)
        inverse = inv_in[s][:, 0:1]
        for i in range(GROUP // BLK):
            cols = slice(i * BLK, (i + 1) * BLK)
            hidden_grad = lax.dot_general(grads, w_block(s, i), NT, preferred_element_type=F32)
            normed = xi[s, :, cols].astype(F32) * inverse
            change = inverse * (hidden_grad * gain_in[s, i:i + 1, :] - normed * inner)
            for j in range(BLK // HD):
                h = i * (BLK // HD) + j
                place = slice(h * SEQ, (h + 1) * SEQ)
                up[place, :] = (
                    up[place, :].astype(F32) + change[:, j * HD:(j + 1) * HD]
                ).astype(BF16)

    def update_last(s):
        grads = vgb[s]
        inverse = inv_in[s][:, 0:1]
        partial = jnp.zeros((SEQ, HD), F32)
        for i in range(GROUP // BLK):
            cols = slice(i * BLK, (i + 1) * BLK)
            hidden_grad = lax.dot_general(grads, w_block(s, i), NT, preferred_element_type=F32)
            scaled = hidden_grad * gain_in[s, i:i + 1, :]
            hg[:, cols] = scaled
            product = scaled * (xi[s, :, cols].astype(F32) * inverse)
            partial += product[:, :HD] + product[:, HD:]
        partial = jnp.sum(partial, axis=1, keepdims=True)
        inner_in[x] = jnp.broadcast_to(partial, (SEQ, HD))
        for k in range(1, NX):
            g = mod(x + k, NX)
            go(
                send(
                    inner_in.at[x], inner_in.at[x], s_in.at[k], r_in.at[x], section=2 * g + c
                )
            )
        for g in peers():
            arrived(inner_in.at[g], r_in.at[g])
        inner = sum(inner_in[g] for g in range(NX))[:, 0:1] * (1.0 / D)
        for h in range(PER):
            cols = slice(h * HD, (h + 1) * HD)
            place = slice(h * SEQ, (h + 1) * SEQ)
            change = inverse * (hg[:, cols] - xi[s, :, cols].astype(F32) * inverse * inner)
            up[place, :] = (up[place, :].astype(F32) + change).astype(BF16)

    def drain_chain():
        @pl.loop(0, LAYERS)
        def _(s):
            for copy in vg_copies(s):
                copy.wait_send()

        @pl.loop(2, LAYERS)
        def _(s):
            for k in range(1, NX):
                v_part(s, k).wait_send()
                v_sum_copy(s, k).wait_send()

        vp_copy(mate).wait_send()

    def vg_rows(yy):
        return vg_all.at[pl.ds(aligned(yy, 2 * SEQ), 2 * SEQ)]

    def send_value_grads():
        vg_all[vg_place(c)] = vgb[sec]
        arrived(vg_all.at[vg_place(1 - c)], r_vp)
        for k in range(1, NY):
            yy = mod(y + k, NY)
            go(send(vg_rows(y), vg_rows(y), s_vy.at[k], r_vy.at[y], replica=at_dp(z, yy)))
        for k in range(1, NY):
            yy = mod(y + k, NY)
            arrived(vg_rows(yy), r_vy.at[yy])

    def product(q, owner):
        return jnp.dot(
            vg_t[q * CUT:(q + 1) * CUT, :], h_all[:, pl.ds(aligned(owner, BLK), BLK)],
            preferred_element_type=F32,
        )

    def rs_copy(way, m, q):
        to = mod(z + 1, NZ) if way == 0 else mod(z - 1, NZ)
        return send(
            rs_send.at[way, m, q], rs_recv.at[way, m, q], s_rs.at[way, m, q],
            r_rs.at[way, m, q], replica=at_dp(to, y),
        )

    def pass_on(way, m, q, joined):
        ahead = HOPS - m
        part = product(q, mod(z + ahead, NZ) if way == 0 else mod(z - ahead, NZ))
        if joined:
            rs_copy(way, m - 1, q).wait_recv()
            part += rs_recv[way, m - 1, q].astype(F32)
        rs_send[way, m, q] = part.astype(BF16)
        go(rs_copy(way, m, q))

    def reduce_products():
        vg_t[...] = vg_all[...].astype(F32).T.astype(BF16)
        far = ((0, 1), (2, 3))
        rest = ((2, 3), (0, 1))
        for i in range(2):
            for way in range(2):
                pass_on(way, 0, far[way][i], False)
        for i in range(2):
            for way in range(2):
                pass_on(way, 1, rest[way][i], False)
        for i in range(2):
            for way in range(2):
                pass_on(way, 1, far[way][i], True)
        for m in range(2, HOPS):
            for group in (rest, far):
                for i in range(2):
                    for way in range(2):
                        pass_on(way, m, group[way][i], True)
        squares_sum = jnp.zeros((1, 1), F32)
        for q in range(STREAMS):
            total[q] = product(q, z)
        for q in (2, 0, 3, 1):
            owned = total[q]
            for way in range(2):
                rs_copy(way, HOPS - 1, q).wait_recv()
                owned += rs_recv[way, HOPS - 1, q].astype(F32)
            total[q] = owned
            part = jnp.sum(owned * owned, axis=1, keepdims=True)
            squares_sum += jnp.sum(part, axis=0, keepdims=True)
        return squares_sum

    def clip(squares_sum):
        stages = (
            (n1, LAYERS, sec, lambda i: (i, dp)),
            (n2, NY, y, lambda i: (sec, at_dp(z, i))),
            (n3, NZ, z, lambda i: (sec, at_dp(i, y))),
        )
        value = jnp.broadcast_to(squares_sum, (8, 128))
        for t, (slots, count, me, place) in enumerate(stages):
            slots[me] = value
            for k in range(1, count):
                section, replica = place(mod(me + k, count))
                go(
                    send(
                        slots.at[me], slots.at[me], s_n.at[t, k], r_n.at[t, me], section=section,
                        replica=replica,
                    )
                )
            for k in range(1, count):
                i = mod(me + k, count)
                arrived(slots.at[i], r_n.at[t, i])
            value = sum(slots[i] for i in range(count))
        ceiling = float(LAYERS * D * KV) ** 0.5
        factor = jnp.minimum(1.0, ceiling / jnp.sqrt(value[0:1, 0:1]))
        for q in range(STREAMS):
            out_ref[:, q * CUT:(q + 1) * CUT] = (total[q] * factor).T

    send_weights()
    send_inputs()
    send_inverse()
    send_probabilities()
    column(3)
    make_hidden()
    column(2)
    row(3)
    finish(3)
    column(1)
    top_ready()
    inputs_ready(7)
    inputs_ready(6)
    weights_ready(3)
    v_start(7)
    v_start(6)
    row(2)
    column(0)
    v_sum(7)
    vg_start(7)
    v_sum(6)
    finish(2)
    v_ready(7)
    vg_ready(7)
    update(7)
    vg_start(6)
    row(1)
    v_ready(6)
    vg_ready(6)
    update(6)
    inputs_ready(5)
    inputs_ready(4)
    weights_ready(2)
    v_start(5)
    v_start(4)
    finish(1)
    row(0)
    send_hidden()
    v_sum(5)
    vg_start(5)
    v_sum(4)
    v_ready(5)
    vg_ready(5)
    update(5)
    vg_start(4)
    finish(0)
    v_ready(4)
    vg_ready(4)
    update(4)
    inputs_ready(3)
    inputs_ready(2)
    inputs_ready(1)
    inputs_ready(0)
    weights_ready(1)
    v_start(3)
    v_start(2)
    v_sum(3)
    vg_start(3)
    v_sum(2)
    v_ready(3)
    vg_ready(3)
    update(3)
    vg_start(2)
    v_ready(2)
    vg_ready(2)
    update(2)
    vg_start(1)
    vg_ready(1)
    weights_ready(0)
    update_last(1)
    vg_start(0)
    vg_ready(0)
    drains.append(drain_chain)
    send_value_grads()
    hidden_ready()
    clip(reduce_products())

    for drain in drains:
        drain()
    for copy, when in pending:
        if when is None:
            copy.wait_send()
        else:
            pl.when(when)(copy.wait_send)


def shards(layer_inputs, queries, keys, gains, value_weights, out_grad):
    dma, vmem = pltpu.SemaphoreType.DMA, pltpu.VMEM
    scratch = [
        vmem((D // BLK, BLK), F32),
        vmem((2 * SEQ, D), BF16),
        vmem((2 * SEQ, D), BF16),
        vmem((2, NX, 2 * NY, BLK, KV), BF16),
        vmem((LAYERS, SEQ, GROUP), BF16),
        vmem((LAYERS, SEQ, STACK), BF16),
        vmem((LAYERS, SEQ, HD), F32),
        vmem((LAYERS, 8, BLK), F32),
        vmem((LAYERS, SEQ, STACK), BF16),
        vmem((2 * SEQ, HD), F32),
        vmem((SEQ, STACK), F32),
        vmem((SEQ, GROUP), BF16),
        vmem((STACK, HD), BF16),
        vmem((LAYERS, SEQ, KV), BF16),
        vmem((LAYERS, NX, SEQ, HD), BF16),
        vmem((LAYERS, NX, SEQ, HD), BF16),
        vmem((LAYERS, SEQ, KV), BF16),
        vmem((SEQ, GROUP), F32),
        vmem((NX, SEQ, HD), F32),
        vmem((NY, 2 * SEQ, GROUP), BF16),
        vmem((NY * 2 * SEQ, GROUP), BF16),
        vmem((NY * 2 * SEQ, KV), BF16),
        vmem((KV, NY * 2 * SEQ), BF16),
        vmem((2, HOPS, STREAMS, CUT, BLK), BF16),
        vmem((2, HOPS, STREAMS, CUT, BLK), BF16),
        vmem((STREAMS, CUT, BLK), F32),
        vmem((LAYERS, 8, 128), F32),
        vmem((NY, 8, 128), F32),
        vmem((NZ, 8, 128), F32),
        dma((8,)),
        dma((LAYERS,)), dma((LAYERS,)),
        dma((LAYERS,)), dma((LAYERS,)),
        dma((LAYERS,)), dma((LAYERS,)),
        dma((LAYERS,)), dma((LAYERS,)),
        dma, dma,
        dma((2,)), dma((NX, 2, 2)), dma((NX, 3, 2)), dma((NX, 2, 2, 2)), dma((NX, 2, 2)),
        dma((NX, 2, NY, 2)),
        dma((NX,)), dma((NX,)),
        dma((LAYERS, NX)), dma((LAYERS, NX)), dma((LAYERS, NX)), dma((LAYERS, NX)),
        dma((NX,)), dma((NX,)),
        dma((LAYERS, NX)), dma((LAYERS, NX)),
        dma, dma,
        dma((NY,)), dma((NY,)),
        dma((NY,)), dma((NY,)),
        dma((2, HOPS, STREAMS)), dma((2, HOPS, STREAMS)),
        dma((3, LAYERS)), dma((3, LAYERS)),
    ]
    hbm, whole = pl.BlockSpec(memory_space=pl.ANY), pl.BlockSpec(memory_space=pltpu.VMEM)
    out = pl.pallas_call(
        body,
        out_shape=jax.ShapeDtypeStruct((BLK, KV), F32),
        in_specs=[hbm, hbm, whole, whole, hbm, hbm],
        out_specs=whole,
        scratch_shapes=scratch,
        compiler_params=pltpu.CompilerParams(
            collective_id=0, has_side_effects=True, vmem_limit_bytes=60 * 1024 * 1024
        ),
    )(layer_inputs[0], queries[0], keys[0], gains, value_weights[0], out_grad)
    return out[None]


def solution(mesh):
    return jax.shard_map(
        shards,
        mesh=mesh,
        in_specs=(
            P("section", "dp", None),
            P("section", "dp", None),
            P("section", "dp", None),
            P("section", None),
            P("section", "dp", None),
            P("dp", "section"),
        ),
        out_specs=P("section", "dp", None),
        check_vma=False,
    )
```

time: 249 us -> 194 us (0.78)
  Pallas kernels: 246 us -> 190 us
    pallas_call x1, Pallas kernels: 246 us -> 190 us  [shards(): pl.pallas_call(body, out_shape=jax.ShapeDtypeStruct((BLK, KV), F32), in_s...]
where the time goes in v2:
time: 194 us; the launch traced here: 192 us
  Pallas kernels  190 us (98%)
    pallas_call x1, Pallas kernels, shards(): pl.pallas_call(body, out_shape=jax.ShapeDtypeStruct((BLK, KV), F32), in_s...  190 us

profile of v2, /device:TPU:1, one launch (start us, length us, event | category | flops | bytes accessed | tf_op | source)
XLA Modules:
  0.0 191.8 jit_solution(10290590643642872686)
XLA Ops:
  0.0 189.9 %shard_map.64 = f32[256,512]{1,0:T(8,128)} custom-call(bf16[160,8192]{1,0:T(8,128)(2,1)} %bitcast.5, bf16[160,8192]{1,0:T(8,128)(2,1)} %bitcast.6, bf16[160,512]{1,0:T(8,128)(2,1)} %bitcast.9, bf16[1,8192]{1,0:T(2,128)(2,1)} %gain_bf.1, bf16[256,512]{1,0:T(8,128)(2,1)} %bitcast.8, bf16[160,1024]{1,0:T(8,128)(2,1)} %og_hbm.1), custom_call_target="tpu_custom_call" | custom-call | tf_op jit(solution)/shard_map/pallas_call | solution.py:650
  189.9 1.9 copy.8

commit v3 on v2

--- a/solution.py
+++ b/solution.py
@@ -34,7 +34,7 @@
     xv, qv, wall, xi, pt, inv_in, gain_in, p_own, inv_own, mask, top, up, vgb, v_own, v_in, v_all, hg, inner_in,
     h_own, h_all, vg_all, vg_t, rs_send, rs_recv, total, n1, n2, n3,
     s_loc, s_x, r_x, s_p, r_p, s_i, r_i, s_g, r_g, s_og, r_og, s_wx, r_w, s_z, s_y, s_yf, r_y,
-    s_pt, r_pt, s_v, r_v, s_w, r_vs, s_in, r_in, s_vg, r_vg, s_vp, r_vp, s_vy, r_vy, s_h, r_h, s_rs, r_rs, s_n, r_n,
+    s_pt, r_pt, s_v, r_v, s_w, r_vs, s_in, r_in, s_vg, r_vg, s_vy, r_vy, s_h, r_h, s_rs, r_rs, s_n, r_n,
 ):
     sec, dp = lax.axis_index("section"), lax.axis_index("dp")
     x, c = lax.div(sec, 2), lax.rem(sec, 2)
@@ -65,6 +65,7 @@
     barrier = pltpu.get_barrier_semaphore()
     friends = [(mod(sec + k, LAYERS), dp) for k in range(1, LAYERS)]
     friends += [(sec, at_dp(z, mod(y + k, NY))) for k in range(1, NY)]
+    friends += [(mate, at_dp(z, mod(y + k, NY))) for k in range(1, NY)]
     friends += [(sec, at_dp(mod(z + k, NZ), y)) for k in range(1, NZ)]
     for section, replica in friends:
         pl.semaphore_signal(
@@ -111,6 +112,10 @@
             )
         pl.when(jnp.logical_and(used, jnp.logical_not(w_away)))(w_local.start)
 
+    def x_copy(k):
+        section, g, b = dest(k)
+        return send(block(x_hbm, b, g), xi.at[sec], s_x.at[k], r_x.at[sec], section=section)
+
     def send_inputs():
         for i in range(D // BLK):
             gain_ref[i:i + 1, :] = gain_bf[:, i * BLK:(i + 1) * BLK].astype(F32)
@@ -120,9 +125,9 @@
         og_local.start()
         for k in range(1, LAYERS):
             section, g, b = dest(k)
-            go(send(block(x_hbm, b, g), xi.at[sec], s_x.at[k], r_x.at[sec], section=section))
+            go(x_copy(k), sec > 0)
             gain = gain_ref.at[pl.ds(aligned(g, 8), 8)]
-            go(send(gain, gain_in.at[sec], s_g.at[k], r_g.at[sec], section=section))
+            go(send(gain, gain_in.at[sec], s_g.at[k], r_g.at[sec], section=section), sec > 0)
         xi_local.start()
         gain_in[sec] = gain_ref[pl.ds(aligned(x, 8), 8)]
 
@@ -177,7 +182,10 @@
         inv_own[...] = jnp.broadcast_to(lax.rsqrt(mean + EPSILON), (2 * SEQ, HD))
         for k in range(1, LAYERS):
             section, g, b = dest(k)
-            go(send(inv_own.at[rows(b)], inv_in.at[sec], s_i.at[k], r_i.at[sec], section=section))
+            copy = send(
+                inv_own.at[rows(b)], inv_in.at[sec], s_i.at[k], r_i.at[sec], section=section
+            )
+            go(copy, sec > 0)
         inv_in[sec] = inv_own[rows(c)]
 
     def make_hidden():
@@ -282,10 +290,11 @@
 
         @pl.when(s != sec)
         def _():
-            arrived(xi.at[s], r_x.at[s])
             arrived(pt.at[s], r_p.at[s])
-            arrived(inv_in.at[s], r_i.at[s])
-            arrived(gain_in.at[s], r_g.at[s])
+            if s > 0:
+                arrived(xi.at[s], r_x.at[s])
+                arrived(inv_in.at[s], r_i.at[s])
+                arrived(gain_in.at[s], r_g.at[s])
 
     def peers():
         return [mod(x + k, NX) for k in range(1, NX)]
@@ -344,8 +353,12 @@
     def vg_place(b):
         return pl.ds(pl.multiple_of(y * 2 * SEQ + b * SEQ, 16), SEQ)
 
-    def vp_copy(s):
-        return send(vgb.at[s], vg_all.at[vg_place(c)], s_vp, r_vp, section=mate)
+    def vy_copy(s, k):
+        rows_here = vg_all.at[vg_place(c)]
+        return send(
+            vgb.at[s], rows_here, s_vy.at[s % 2, k], r_vy.at[y, c], section=s,
+            replica=at_dp(z, mod(y + k, NY)),
+        )
 
     def vg_start(s):
         grad = jnp.dot(pt[s], up[...], preferred_element_type=F32).astype(BF16)
@@ -356,7 +369,13 @@
     def vg_ready(s):
         for g in peers():
             arrived(vg_cols(s, g), r_vg.at[s, g])
-        pl.when(mate == s)(lambda: vp_copy(s).start())
+
+        @pl.when(x == s // 2)
+        def _():
+            for k in range(1, NY):
+                vy_copy(s, k).start()
+
+        pl.when(mate == s)(lambda: vy_copy(s, 0).start())
 
     def update(s):
         grads = vgb[s]
@@ -416,20 +435,18 @@
                 v_part(s, k).wait_send()
                 v_sum_copy(s, k).wait_send()
 
-        vp_copy(mate).wait_send()
-
-    def vg_rows(yy):
-        return vg_all.at[pl.ds(aligned(yy, 2 * SEQ), 2 * SEQ)]
-
-    def send_value_grads():
+        for k in range(1, NY):
+            vy_copy(sec, k).wait_send()
+            vy_copy(mate, k).wait_send()
+        vy_copy(mate, 0).wait_send()
+
+    def value_grads_ready():
         vg_all[vg_place(c)] = vgb[sec]
-        arrived(vg_all.at[vg_place(1 - c)], r_vp)
-        for k in range(1, NY):
+        for k in range(NY):
             yy = mod(y + k, NY)
-            go(send(vg_rows(y), vg_rows(y), s_vy.at[k], r_vy.at[y], replica=at_dp(z, yy)))
-        for k in range(1, NY):
-            yy = mod(y + k, NY)
-            arrived(vg_rows(yy), r_vy.at[yy])
+            for b in (1 - c,) if k == 0 else (0, 1):
+                place = pl.ds(pl.multiple_of(yy * 2 * SEQ + b * SEQ, 16), SEQ)
+                arrived(vg_all.at[place], r_vy.at[yy, b])
 
     def product(q, owner):
         return jnp.dot(
@@ -523,13 +540,13 @@
     top_ready()
     inputs_ready(7)
     inputs_ready(6)
+    vg_start(7)
     weights_ready(3)
     v_start(7)
     v_start(6)
     row(2)
     column(0)
     v_sum(7)
-    vg_start(7)
     v_sum(6)
     finish(2)
     v_ready(7)
@@ -542,6 +559,7 @@
     update(6)
     inputs_ready(5)
     inputs_ready(4)
+    vg_start(5)
     weights_ready(2)
     v_start(5)
     v_start(4)
@@ -549,7 +567,6 @@
     row(0)
     send_hidden()
     v_sum(5)
-    vg_start(5)
     v_sum(4)
     v_ready(5)
     vg_ready(5)
@@ -563,11 +580,11 @@
     inputs_ready(2)
     inputs_ready(1)
     inputs_ready(0)
+    vg_start(3)
     weights_ready(1)
     v_start(3)
     v_start(2)
     v_sum(3)
-    vg_start(3)
     v_sum(2)
     v_ready(3)
     vg_ready(3)
@@ -583,7 +600,7 @@
     vg_start(0)
     vg_ready(0)
     drains.append(drain_chain)
-    send_value_grads()
+    value_grads_ready()
     hidden_ready()
     clip(reduce_products())
 
@@ -640,8 +657,7 @@
         dma((LAYERS, NX)), dma((LAYERS, NX)), dma((LAYERS, NX)), dma((LAYERS, NX)),
         dma((NX,)), dma((NX,)),
         dma((LAYERS, NX)), dma((LAYERS, NX)),
-        dma, dma,
-        dma((NY,)), dma((NY,)),
+        dma((2, NY)), dma((NY, 2)),
         dma((NY,)), dma((NY,)),
         dma((2, HOPS, STREAMS)), dma((2, HOPS, STREAMS)),
         dma((3, LAYERS)), dma((3, LAYERS)),

time: 194 us -> 187 us (0.964)
  Pallas kernels: 190 us -> 183 us
    pallas_call x1, Pallas kernels: 190 us -> 183 us  [shards(): pl.pallas_call(body, out_shape=jax.ShapeDtypeStruct((BLK, KV), F32), in_s...]
where the time goes in v3:
time: 187 us; the launch traced here: 185 us
  Pallas kernels  183 us (98%)
  local copies, waits for them, and re-layouts  1.87 us (1%)
    pallas_call x1, Pallas kernels, shards(): pl.pallas_call(body, out_shape=jax.ShapeDtypeStruct((BLK, KV), F32), in_s...  183 us

profile of v3, /device:TPU:1, one launch (start us, length us, event | category | flops | bytes accessed | tf_op | source)
XLA Modules:
  0.0 184.9 jit_solution(10050658125059441779)
XLA Ops:
  0.0 183.0 %shard_map.64 = f32[256,512]{1,0:T(8,128)} custom-call(bf16[160,8192]{1,0:T(8,128)(2,1)} %bitcast.5, bf16[160,8192]{1,0:T(8,128)(2,1)} %bitcast.6, bf16[160,512]{1,0:T(8,128)(2,1)} %bitcast.9, bf16[1,8192]{1,0:T(2,128)(2,1)} %gain_bf.1, bf16[256,512]{1,0:T(8,128)(2,1)} %bitcast.8, bf16[160,1024]{1,0:T(8,128)(2,1)} %og_hbm.1), custom_call_target="tpu_custom_call" | custom-call | tf_op jit(solution)/shard_map/pallas_call | solution.py:666
  183.0 1.9 %copy.8 = f32[1,256,512]{2,1,0:T(8,128)} copy(f32[1,256,512]{2,1,0:T(8,128)} %bitcast.7) | data formatting | bytes 1048576

commit v4 on v3

--- a/solution.py
+++ b/solution.py
@@ -32,7 +32,7 @@
 def body(
     x_hbm, q_hbm, k_ref, gain_bf, w_hbm, og_hbm, out_ref, gain_ref,
     xv, qv, wall, xi, pt, inv_in, gain_in, p_own, inv_own, mask, top, up, vgb, v_own, v_in, v_all, hg, inner_in,
-    h_own, h_all, vg_all, vg_t, rs_send, rs_recv, total, n1, n2, n3,
+    h_own, h_all, vg_all, vg_t, rs_send, rs_recv, total, n1, n3,
     s_loc, s_x, r_x, s_p, r_p, s_i, r_i, s_g, r_g, s_og, r_og, s_wx, r_w, s_z, s_y, s_yf, r_y,
     s_pt, r_pt, s_v, r_v, s_w, r_vs, s_in, r_in, s_vg, r_vg, s_vy, r_vy, s_h, r_h, s_rs, r_rs, s_n, r_n,
 ):
@@ -65,7 +65,8 @@
     barrier = pltpu.get_barrier_semaphore()
     friends = [(mod(sec + k, LAYERS), dp) for k in range(1, LAYERS)]
     friends += [(sec, at_dp(z, mod(y + k, NY))) for k in range(1, NY)]
-    friends += [(mate, at_dp(z, mod(y + k, NY))) for k in range(1, NY)]
+    for i in range(1, LAYERS):
+        friends += [(mod(sec + i, LAYERS), at_dp(z, mod(y + k, NY))) for k in range(1, NY)]
     friends += [(sec, at_dp(mod(z + k, NZ), y)) for k in range(1, NZ)]
     for section, replica in friends:
         pl.semaphore_signal(
@@ -503,8 +504,7 @@
 
     def clip(squares_sum):
         stages = (
-            (n1, LAYERS, sec, lambda i: (i, dp)),
-            (n2, NY, y, lambda i: (sec, at_dp(z, i))),
+            (n1, LAYERS * NY, sec * NY + y, lambda i: (lax.div(i, NY), at_dp(z, lax.rem(i, NY)))),
             (n3, NZ, z, lambda i: (sec, at_dp(i, y))),
         )
         value = jnp.broadcast_to(squares_sum, (8, 128))
@@ -642,8 +642,7 @@
         vmem((2, HOPS, STREAMS, CUT, BLK), BF16),
         vmem((2, HOPS, STREAMS, CUT, BLK), BF16),
         vmem((STREAMS, CUT, BLK), F32),
-        vmem((LAYERS, 8, 128), F32),
-        vmem((NY, 8, 128), F32),
+        vmem((LAYERS * NY, 8, 128), F32),
         vmem((NZ, 8, 128), F32),
         dma((8,)),
         dma((LAYERS,)), dma((LAYERS,)),
@@ -660,7 +659,7 @@
         dma((2, NY)), dma((NY, 2)),
         dma((NY,)), dma((NY,)),
         dma((2, HOPS, STREAMS)), dma((2, HOPS, STREAMS)),
-        dma((3, LAYERS)), dma((3, LAYERS)),
+        dma((2, LAYERS * NY)), dma((2, LAYERS * NY)),
     ]
     hbm, whole = pl.BlockSpec(memory_space=pl.ANY), pl.BlockSpec(memory_space=pltpu.VMEM)
     out = pl.pallas_call(

time: 187 us -> 185 us (0.989); the launches traced: 185 us -> 185 us
  no operation moved by 1% of the time
where the time goes in v4:
time: 185 us
  Pallas kernels  183 us (99%)
  local copies, waits for them, and re-layouts  1.87 us (1%)
    pallas_call x1, Pallas kernels, shards(): pl.pallas_call(body, out_shape=jax.ShapeDtypeStruct((BLK, KV), F32), in_s...  183 us

profile of v4, /device:TPU:1, one launch (start us, length us, event | category | flops | bytes accessed | tf_op | source)
XLA Modules:
  0.0 185.3 jit_solution(16015144595287396765)
XLA Ops:
  0.0 183.4 %shard_map.64 = f32[256,512]{1,0:T(8,128)} custom-call(bf16[160,8192]{1,0:T(8,128)(2,1)} %bitcast.5, bf16[160,8192]{1,0:T(8,128)(2,1)} %bitcast.6, bf16[160,512]{1,0:T(8,128)(2,1)} %bitcast.9, bf16[1,8192]{1,0:T(2,128)(2,1)} %gain_bf.1, bf16[256,512]{1,0:T(8,128)(2,1)} %bitcast.8, bf16[160,1024]{1,0:T(8,128)(2,1)} %og_hbm.1), custom_call_target="tpu_custom_call" | custom-call | tf_op jit(solution)/shard_map/pallas_call | solution.py:665
  183.5 1.9 %copy.8 = f32[1,256,512]{2,1,0:T(8,128)} copy(f32[1,256,512]{2,1,0:T(8,128)} %bitcast.7) | data formatting | bytes 1048576
